TPU v7x, 32 devices: a whole 2x2x4 slice. The times are simulated.
32 devices in a mesh: tour: 8 (over y, x, core), width: 4 (over z).
Axes of the slice: x: 2, y: 2, z: 4, core: 2. Of those that a mesh axis runs over, the one named last changes fastest.
Arguments:
- images: bfloat16 [2048, 1152], P('tour', 'width'), may hold values from -1.1953125 to 1.1953125
- texts: bfloat16 [2048, 1152], P('tour', 'width'), may hold values from -1.1953125 to 1.1953125
- matches: int32 [8, 256], P('tour'), may hold values from 0 to 255, each once within a row
- scale: float32 [1], replicated, may hold values from 0.7 to 2.5
- shift_bias: float32 [1], replicated, may hold values from -3 to 0
Outputs:
- grad_images: float32 [2048, 1152], P('tour', 'width')
- grad_texts: float32 [2048, 1152], P('tour', 'width')
All inputs are finite; a program needn't handle non-finite values.
Results may differ from a plain program's by a relative error of at most 0.0025.
Values may be sent and summed in bfloat16 or wider, within the bound.
A program may use at most 64 MiB of HBM per device.

v0:
```python
import jax
import jax.numpy as jnp
from jax import lax
from jax.sharding import PartitionSpec as P

REACH = 7


def shifted(block, axis, distance):
    devices = range(lax.axis_size(axis))
    route = [((i - distance) % len(devices), i) for i in devices]
    return lax.ppermute(block, axis, route)


def cross_rows(left, right):
    return lax.dot_general(
        left, right, (((1,), (1,)), ((), ())), preferred_element_type=jnp.float32
    )


def cross_cols(weights, right):
    return lax.dot_general(
        weights, right, (((0,), (0,)), ((), ())), preferred_element_type=jnp.float32
    )


def per_device(images, texts, matches, scale, shift_bias):
    temper = scale[0]
    offset_bias = shift_bias[0]
    rows = images.shape[0]
    columns = lax.broadcasted_iota(jnp.int32, (rows, rows), 1)
    positive = (columns == matches[0][:, None]).astype(jnp.float32)

    def to_weights(total, label):
        probs = jax.nn.sigmoid(temper * total + offset_bias)
        if label is not None:
            probs = probs - label
        return probs.astype(jnp.bfloat16)

    def finish(parts, labels):
        totals = lax.psum(parts, "width")
        return tuple((to_weights(total, label) for total, label in zip(totals, labels)))

    own = finish((cross_rows(images, texts),), (positive,))[0]
    grad_image = jnp.dot(own, texts, preferred_element_type=jnp.float32)
    grad_text = cross_cols(own, images)
    for step in range(1, REACH + 1):
        lower = shifted(texts, "tour", step)
        upper = shifted(texts, "tour", -step)
        weight_low, weight_up = finish(
            (cross_rows(images, lower), cross_rows(images, upper)), (None, None)
        )
        grad_image = grad_image + jnp.dot(weight_low, lower, preferred_element_type=jnp.float32)
        grad_image = grad_image + jnp.dot(weight_up, upper, preferred_element_type=jnp.float32)
        back_low = shifted(cross_cols(weight_low, images), "tour", -step)
        back_up = shifted(cross_cols(weight_up, images), "tour", step)
        grad_text = grad_text + back_low + back_up
    return (temper * grad_image, temper * grad_text)


def solution(mesh):
    placed = (P("tour", "width"), P("tour", "width"), P("tour", None), P(), P())
    return jax.shard_map(
        per_device,
        mesh=mesh,
        in_specs=placed,
        out_specs=(P("tour", "width"), P("tour", "width")),
        check_vma=False,
    )
```

profile of v0, /device:TPU:0, one launch (start us, length us, event | category | flops | bytes accessed | tf_op | source)
XLA Modules:
  0.0 159.7 jit_solution(15336267757407937833)
XLA Ops:
  7.7 2.9 %collective-permute-start.1 = (bf16[256,288]{0,1:T(8,128)(2,1)}, bf16[256,288]{0,1:T(8,128)(2,1)S(1)}, u32[]{:S(2)}, u32[]{:S(2)}) collective-permute-start(bf16[256,288]{0,1:T(8,128)(2,1)} %param.6), channel_id=1, source_target_pairs={{4,0},{8,4},{12,8},{16,12},{20,16},{24,20},{28,24},{0,28},{5,1},{9... | collective-permute-start | bytes 442376 | tf_op jit(solution)/shard_map/ppermute | solution.py:12
  10.7 1.3 collective-permute-start.2
  12.0 1.6 %collective-permute-start.3 = (bf16[256,288]{0,1:T(8,128)(2,1)}, bf16[256,288]{0,1:T(8,128)(2,1)S(1)}, u32[]{:S(2)}, u32[]{:S(2)}) collective-permute-start(bf16[256,288]{0,1:T(8,128)(2,1)} %param.6), channel_id=1, source_target_pairs={{8,0},{12,4},{16,8},{20,12},{24,16},{28,20},{0,24},{4,28},{9,1},{1... | collective-permute-start | bytes 442376 | tf_op jit(solution)/shard_map/ppermute | solution.py:12
  13.6 1.9 %fusion.42 = f32[256,256]{1,0:T(8,128)} fusion(bf16[256,288]{0,1:T(8,128)(2,1)S(1)} %copy-done, bf16[256,288]{0,1:T(8,128)(2,1)} %param.6), kind=kOutput, calls=%fused_computation.53 | convolution fusion | flops 37748736 | bytes 557056 | tf_op jit(solution)/shard_map/dot_general | solution.py:16
  15.6 1.7 %collective-permute-start.5 = (bf16[256,288]{0,1:T(8,128)(2,1)S(1)}, bf16[256,288]{0,1:T(8,128)(2,1)S(1)}, u32[]{:S(2)}, u32[]{:S(2)}) collective-permute-start(bf16[256,288]{0,1:T(8,128)(2,1)S(1)} %copy-done.2), channel_id=1, source_target_pairs={{12,0},{16,4},{20,8},{24,12},{28,16},{0,20},{4,24},{8,28},{13,1},{... | collective-permute-start | bytes 442376 | tf_op jit(solution)/shard_map/ppermute | solution.py:12
  17.3 1.0 fusion.43
  18.2 2.2 %collective-permute-start.6 = (bf16[256,288]{0,1:T(8,128)(2,1)S(1)}, bf16[256,288]{0,1:T(8,128)(2,1)S(1)}, u32[]{:S(2)}, u32[]{:S(2)}) collective-permute-start(bf16[256,288]{0,1:T(8,128)(2,1)S(1)} %copy-done.2), channel_id=1, source_target_pairs={{16,0},{20,4},{24,8},{28,12},{0,16},{4,20},{8,24},{12,28},{17,1},{... | collective-permute-start | bytes 442376 | tf_op jit(solution)/shard_map/ppermute | solution.py:12
  20.5 1.0 fusion.44
  23.2 1.0 fusion.46
  24.1 1.0 fusion.47
  25.1 1.0 fusion.48
  26.1 1.2 collective-permute-done.6
  27.4 1.0 fusion.49
  29.7 89.8 %all-reduce.3.cloned.1.call-done = (f32[256,256]{1,0:T(8,128)}, f32[256,256]{1,0:T(8,128)}, f32[256,256]{1,0:T(8,128)}, f32[256,256]{1,0:T(8,128)}, f32[256,256]...) async-done(((f32[256,256]{1,0:T(8,128)}, f32[256,256]{1,0:T(8,128)}, f32[256,256]{1,0:T(8,128)}, f32[256,256]{1,0:T(8,128)}, ...) | async-done | bytes 2097168 | tf_op jit(solution)/shard_map/psum | solution.py:41
  119.4 1.2 fusion.28
  120.7 1.9 %collective-permute-start.7 = (f32[256,288]{0,1:T(8,128)S(1)}, f32[256,288]{0,1:T(8,128)S(1)}, u32[]{:S(2)}, u32[]{:S(2)}) collective-permute-start(f32[256,288]{0,1:T(8,128)S(1)} %fusion.28), channel_id=1, source_target_pairs={{4,0},{8,4},{12,8},{16,12},{20,16},{24,20},{28,24},{0,28},{5,1},{9... | collective-permute-start | bytes 884744 | tf_op jit(solution)/shard_map/ppermute | solution.py:12
  124.7 1.4 collective-permute-start.10
  130.7 1.2 collective-permute-start.12
  132.0 1.2 collective-permute-done.8
  134.6 1.2 fusion.15
  136.3 6.3 %collective-permute-done.10 = f32[256,288]{0,1:T(8,128)S(1)} collective-permute-done((f32[256,288]{0,1:T(8,128)S(1)}, f32[256,288]{0,1:T(8,128)S(1)}, u32[]{:S(2)}, u32[]{:S(2)}) %collective-permute-start.10) | collective-permute-done | bytes 294944 | tf_op jit(solution)/shard_map/ppermute | solution.py:12
  142.6 6.5 %collective-permute-done.11 = f32[256,288]{0,1:T(8,128)S(1)} collective-permute-done((f32[256,288]{0,1:T(8,128)S(1)}, f32[256,288]{0,1:T(8,128)S(1)}, u32[]{:S(2)}, u32[]{:S(2)}) %collective-permute-start.11) | collective-permute-done | bytes 294944 | tf_op jit(solution)/shard_map/ppermute | solution.py:12
  149.6 2.1 %collective-permute-done.13 = f32[256,288]{0,1:T(8,128)S(1)} collective-permute-done((f32[256,288]{0,1:T(8,128)S(1)}, f32[256,288]{0,1:T(8,128)S(1)}, u32[]{:S(2)}, u32[]{:S(2)}) %collective-permute-start.13) | collective-permute-done | bytes 294944 | tf_op jit(solution)/shard_map/ppermute | solution.py:12
  151.8 1.1 fusion.27
  (53 shorter events, 11.5 us)
Async XLA Ops:
  7.2 6.5 %copy-start = (bf16[256,288]{0,1:T(8,128)(2,1)S(1)}, bf16[256,288]{0,1:T(8,128)(2,1)}, u32[]{:S(2)}) copy-start(bf16[256,288]{0,1:T(8,128)(2,1)} %param.5) | copy-start | bytes 442372
  7.2 8.4 %copy-start.2 = (bf16[256,288]{0,1:T(8,128)(2,1)S(1)}, bf16[256,288]{0,1:T(8,128)(2,1)}, u32[]{:S(2)}) copy-start(bf16[256,288]{0,1:T(8,128)(2,1)} %param.6) | copy-start | bytes 442372
  7.2 112.3 %all-reduce.3.cloned.1.call-start = ((), (), s32[]{:S(2)}) async-start(), calls=%async_computation | async-start | bytes 4194304 | tf_op jit(solution)/shard_map/psum | solution.py:41
  7.2 8.3 %collective-permute-start = (bf16[256,288]{0,1:T(8,128)(2,1)}, bf16[256,288]{0,1:T(8,128)(2,1)S(1)}, u32[]{:S(2)}, u32[]{:S(2)}) collective-permute-start(bf16[256,288]{0,1:T(8,128)(2,1)} %param.6), channel_id=1, source_target_pairs={{28,0},{0,4},{4,8},{8,12},{12,16},{16,20},{20,24},{24,28},{29,1},{... | collective-permute-start | bytes 442376 | tf_op jit(solution)/shard_map/ppermute | solution.py:12
  7.7 10.5 %collective-permute-start.1 = (bf16[256,288]{0,1:T(8,128)(2,1)}, bf16[256,288]{0,1:T(8,128)(2,1)S(1)}, u32[]{:S(2)}, u32[]{:S(2)}) collective-permute-start(bf16[256,288]{0,1:T(8,128)(2,1)} %param.6), channel_id=1, source_target_pairs={{4,0},{8,4},{12,8},{16,12},{20,16},{24,20},{28,24},{0,28},{5,1},{9... | collective-permute-start | bytes 442376 | tf_op jit(solution)/shard_map/ppermute | solution.py:12
  10.7 10.7 %collective-permute-start.2 = (bf16[256,288]{0,1:T(8,128)(2,1)}, bf16[256,288]{0,1:T(8,128)(2,1)S(1)}, u32[]{:S(2)}, u32[]{:S(2)}) collective-permute-start(bf16[256,288]{0,1:T(8,128)(2,1)} %param.6), channel_id=1, source_target_pairs={{24,0},{28,4},{0,8},{4,12},{8,16},{12,20},{16,24},{20,28},{25,1},{... | collective-permute-start | bytes 442376 | tf_op jit(solution)/shard_map/ppermute | solution.py:12
  12.0 11.2 %collective-permute-start.3 = (bf16[256,288]{0,1:T(8,128)(2,1)}, bf16[256,288]{0,1:T(8,128)(2,1)S(1)}, u32[]{:S(2)}, u32[]{:S(2)}) collective-permute-start(bf16[256,288]{0,1:T(8,128)(2,1)} %param.6), channel_id=1, source_target_pairs={{8,0},{12,4},{16,8},{20,12},{24,16},{28,20},{0,24},{4,28},{9,1},{1... | collective-permute-start | bytes 442376 | tf_op jit(solution)/shard_map/ppermute | solution.py:12
  13.6 10.5 %collective-permute-start.4 = (bf16[256,288]{0,1:T(8,128)(2,1)}, bf16[256,288]{0,1:T(8,128)(2,1)S(1)}, u32[]{:S(2)}, u32[]{:S(2)}) collective-permute-start(bf16[256,288]{0,1:T(8,128)(2,1)} %param.6), channel_id=1, source_target_pairs={{20,0},{24,4},{28,8},{0,12},{4,16},{8,20},{12,24},{16,28},{21,1},{... | collective-permute-start | bytes 442376 | tf_op jit(solution)/shard_map/ppermute | solution.py:12
  15.6 9.6 %collective-permute-start.5 = (bf16[256,288]{0,1:T(8,128)(2,1)S(1)}, bf16[256,288]{0,1:T(8,128)(2,1)S(1)}, u32[]{:S(2)}, u32[]{:S(2)}) collective-permute-start(bf16[256,288]{0,1:T(8,128)(2,1)S(1)} %copy-done.2), channel_id=1, source_target_pairs={{12,0},{16,4},{20,8},{24,12},{28,16},{0,20},{4,24},{8,28},{13,1},{... | collective-permute-start | bytes 442376 | tf_op jit(solution)/shard_map/ppermute | solution.py:12
  18.2 9.1 %collective-permute-start.6 = (bf16[256,288]{0,1:T(8,128)(2,1)S(1)}, bf16[256,288]{0,1:T(8,128)(2,1)S(1)}, u32[]{:S(2)}, u32[]{:S(2)}) collective-permute-start(bf16[256,288]{0,1:T(8,128)(2,1)S(1)} %copy-done.2), channel_id=1, source_target_pairs={{16,0},{20,4},{24,8},{28,12},{0,16},{4,20},{8,24},{12,28},{17,1},{... | collective-permute-start | bytes 442376 | tf_op jit(solution)/shard_map/ppermute | solution.py:12
  119.4 3.1 %copy-start.9 = (f32[256,256]{1,0:T(8,128)S(1)}, f32[256,256]{1,0:T(8,128)}, u32[]{:S(2)}) copy-start(f32[256,256]{1,0:T(8,128)} %get-tuple-element.3) | copy-start | bytes 786436
  120.7 10.0 %collective-permute-start.7 = (f32[256,288]{0,1:T(8,128)S(1)}, f32[256,288]{0,1:T(8,128)S(1)}, u32[]{:S(2)}, u32[]{:S(2)}) collective-permute-start(f32[256,288]{0,1:T(8,128)S(1)} %fusion.28), channel_id=1, source_target_pairs={{4,0},{8,4},{12,8},{16,12},{20,16},{24,20},{28,24},{0,28},{5,1},{9... | collective-permute-start | bytes 884744 | tf_op jit(solution)/shard_map/ppermute | solution.py:12
  122.6 1.0 copy-start.8
  122.8 10.3 %collective-permute-start.8 = (f32[256,288]{0,1:T(8,128)S(1)}, f32[256,288]{0,1:T(8,128)S(1)}, u32[]{:S(2)}, u32[]{:S(2)}) collective-permute-start(f32[256,288]{0,1:T(8,128)S(1)} %fusion.30), channel_id=1, source_target_pairs={{28,0},{0,4},{4,8},{8,12},{12,16},{16,20},{20,24},{24,28},{29,1},{... | collective-permute-start | bytes 884744 | tf_op jit(solution)/shard_map/ppermute | solution.py:12
  123.5 0.9 copy-start.7
  123.8 12.5 %collective-permute-start.9 = (f32[256,288]{0,1:T(8,128)S(1)}, f32[256,288]{0,1:T(8,128)S(1)}, u32[]{:S(2)}, u32[]{:S(2)}) collective-permute-start(f32[256,288]{0,1:T(8,128)S(1)} %fusion.32), channel_id=1, source_target_pairs={{8,0},{12,4},{16,8},{20,12},{24,16},{28,20},{0,24},{4,28},{9,1},{1... | collective-permute-start | bytes 884744 | tf_op jit(solution)/shard_map/ppermute | solution.py:12
  124.5 1.7 %copy-start.6 = (f32[256,256]{1,0:T(8,128)S(1)}, f32[256,256]{1,0:T(8,128)}, u32[]{:S(2)}) copy-start(f32[256,256]{1,0:T(8,128)} %get-tuple-element.6) | copy-start | bytes 786436
  124.7 17.9 %collective-permute-start.10 = (f32[256,288]{0,1:T(8,128)S(1)}, f32[256,288]{0,1:T(8,128)S(1)}, u32[]{:S(2)}, u32[]{:S(2)}) collective-permute-start(f32[256,288]{0,1:T(8,128)S(1)} %fusion.34), channel_id=1, source_target_pairs={{24,0},{28,4},{0,8},{4,12},{8,16},{12,20},{16,24},{20,28},{25,1},{... | collective-permute-start | bytes 884744 | tf_op jit(solution)/shard_map/ppermute | solution.py:12
  126.1 1.2 copy-start.5
  126.4 22.7 %collective-permute-start.11 = (f32[256,288]{0,1:T(8,128)S(1)}, f32[256,288]{0,1:T(8,128)S(1)}, u32[]{:S(2)}, u32[]{:S(2)}) collective-permute-start(f32[256,288]{0,1:T(8,128)S(1)} %fusion.36), channel_id=1, source_target_pairs={{12,0},{16,4},{20,8},{24,12},{28,16},{0,20},{4,24},{8,28},{13,1},{... | collective-permute-start | bytes 884744 | tf_op jit(solution)/shard_map/ppermute | solution.py:12
  127.3 1.0 copy-start.4
  128.3 0.9 copy-start.10
  130.7 18.9 %collective-permute-start.12 = (f32[256,288]{0,1:T(8,128)S(1)}, f32[256,288]{0,1:T(8,128)S(1)}, u32[]{:S(2)}, u32[]{:S(2)}) collective-permute-start(f32[256,288]{0,1:T(8,128)S(1)} %fusion.38), channel_id=1, source_target_pairs={{20,0},{24,4},{28,8},{0,12},{4,16},{8,20},{12,24},{16,28},{21,1},{... | collective-permute-start | bytes 884744 | tf_op jit(solution)/shard_map/ppermute | solution.py:12
  133.1 18.6 %collective-permute-start.13 = (f32[256,288]{0,1:T(8,128)S(1)}, f32[256,288]{0,1:T(8,128)S(1)}, u32[]{:S(2)}, u32[]{:S(2)}) collective-permute-start(f32[256,288]{0,1:T(8,128)S(1)} %fusion.40), channel_id=1, source_target_pairs={{16,0},{20,4},{24,8},{28,12},{0,16},{4,20},{8,24},{12,28},{17,1},{... | collective-permute-start | bytes 884744 | tf_op jit(solution)/shard_map/ppermute | solution.py:12
  (2 other events, 1.7 us)
Sparse Core Ops, SparseCore 0:
  28.5 90.9 all-reduce.2
where the time goes:
time: 162 us; the launch traced here: 160 us
  waiting for transfers between devices  109 us (67%)
  starting transfers between devices  17.1 us (11%)
  between operations  15.5 us (10%)
  matrix products  15.3 us (9%)
  local copies, waits for them, and re-layouts  2.9 us (2%)
    psum x1, waiting for transfers between devices, finish(): totals = lax.psum(parts, 'width')  89.8 us
    ppermute x14, waiting for transfers between devices, shifted(): return lax.ppermute(block, axis, route)  19.1 us
    ppermute x14, starting transfers between devices, shifted(): return lax.ppermute(block, axis, route)  17 us
    dot_general x8, matrix products, cross_rows(): lax.dot_general(left, right, (((1,), (1,)), ((), ())), preferred_element_...  8.75 us
    dot_general x8, matrix products, cross_cols(): lax.dot_general(weights, right, (((0,), (0,)), ((), ())), preferred_eleme...  3.74 us
  transfers between devices with their start and end apart: 15, of which 9 were waited for; matrix products, arithmetic and copies ran while one was open for 8% of the time, Pallas kernels for 0%

commit v1 on v0

--- a/solution.py
+++ b/solution.py
@@ -24,7 +24,7 @@
     )
 
 
-def per_device(images, texts, matches, scale, shift_bias):
+def band(images, texts, matches, scale, shift_bias):
     temper = scale[0]
     offset_bias = shift_bias[0]
     rows = images.shape[0]
@@ -58,10 +58,35 @@
     return (temper * grad_image, temper * grad_text)
 
 
+def whole(images, texts, matches, scale, shift_bias):
+    n = lax.axis_size("tour")
+    rows = images.shape[0]
+    temper = scale[0]
+    me = lax.axis_index("tour")
+    gathered = lax.all_gather(texts, "tour", axis=0, tiled=True)
+    total = lax.psum(cross_rows(images, gathered), "width")
+    column = lax.broadcasted_iota(jnp.int32, total.shape, 1)
+    hit = column == matches[0][:, None] + me * rows
+    probs = jax.nn.sigmoid(temper * total + shift_bias[0])
+    weights = (probs - hit.astype(jnp.float32)).astype(jnp.bfloat16)
+    away = (me - column // rows + n) % n
+    times = jnp.ones(total.shape, jnp.bfloat16)
+    for d in range(n):
+        count = len([s for s in range(-REACH, REACH + 1) if s % n == d])
+        times = jnp.where(away == d, jnp.bfloat16(count), times)
+    weights = weights * times
+    grad_image = jnp.dot(weights, gathered, preferred_element_type=jnp.float32)
+    grad_text = lax.psum_scatter(
+        cross_cols(weights, images), "tour", scatter_dimension=0, tiled=True
+    )
+    return (temper * grad_image, temper * grad_text)
+
+
 def solution(mesh):
     placed = (P("tour", "width"), P("tour", "width"), P("tour", None), P(), P())
+    body = whole if mesh.shape["tour"] <= 2 * REACH + 1 else band
     return jax.shard_map(
-        per_device,
+        body,
         mesh=mesh,
         in_specs=placed,
         out_specs=(P("tour", "width"), P("tour", "width")),

time: 162 us -> 181 us (1.12); the launches traced: 160 us -> 181 us
  waiting for transfers between devices: 109 us -> 154 us
  starting transfers between devices: 17.1 us -> 0.12 us
  matrix products: 15.3 us -> 6.42 us
  other arithmetic: 0 us -> 3.87 us
    reduce_scatter x0 -> x1, waiting for transfers between devices: none -> 39.1 us  [whole(): lax.psum_scatter(cross_cols(weights, images), 'tour', scatter_dimension=0...]
    all_gather x0 -> x1, waiting for transfers between devices: none -> 28.8 us  [whole(): gathered = lax.all_gather(texts, 'tour', axis=0, tiled=True)]
    ppermute x14 -> x0, waiting for transfers between devices: 19.1 us -> none  [shifted(): return lax.ppermute(block, axis, route)]
    ppermute x14 -> x0, starting transfers between devices: 17 us -> none  [shifted(): return lax.ppermute(block, axis, route)]
    dot_general x8 -> x1, matrix products: 8.75 us -> 3.31 us  [cross_rows(): lax.dot_general(left, right, (((1,), (1,)), ((), ())), preferred_element_...]
    psum x1, waiting for transfers between devices: 89.8 us -> 85.3 us  [whole(): total = lax.psum(cross_rows(images, gathered), 'width')]
    mul x0 -> x2, other arithmetic: none -> 3.85 us  [the longest x1 2.16 us: whole(): weights = weights * times]
    dot_general x8 -> x1, matrix products: 3.74 us -> 1.88 us  [cross_cols(): lax.dot_general(weights, right, (((0,), (0,)), ((), ())), preferred_eleme...]
  transfers between devices with their start and end apart: 15 -> 3, of which waited for: 9 -> 3; matrix products, arithmetic and copies ran while one was open for 8% -> 1% of each run, Pallas kernels for 0% -> 0%
where the time goes in v1:
time: 181 us
  waiting for transfers between devices  154 us (85%)
  between operations  15.1 us (8%)
  matrix products  6.42 us (4%)
  other arithmetic  3.87 us (2%)
    psum x1, waiting for transfers between devices, whole(): total = lax.psum(cross_rows(images, gathered), 'width')  85.3 us
    reduce_scatter x1, waiting for transfers between devices, whole(): lax.psum_scatter(cross_cols(weights, images), 'tour', scatter_dimension=0...  39.1 us
    all_gather x1, waiting for transfers between devices, whole(): gathered = lax.all_gather(texts, 'tour', axis=0, tiled=True)  28.8 us
  transfers between devices with their start and end apart: 3, of which 3 were waited for; matrix products, arithmetic and copies ran while one was open for 1% of the time, Pallas kernels for 0%

profile of v1, /device:TPU:0, one launch (start us, length us, event | category | flops | bytes accessed | tf_op | source)
XLA Modules:
  0.0 180.7 jit_solution(2274039663072871939)
XLA Ops:
  7.2 0.0 copy-start
  7.2 0.0 all-gather.2.cloned.1.call-start
  7.2 0.7 all-gather.2.cloned.1.call-update
  7.9 0.0 copy-start.2
  7.9 0.0 all-reduce.2.cloned.1.call-start
  8.0 28.8 %all-gather.2.cloned.1.call-done = bf16[2048,288]{0,1:T(8,128)(2,1)} async-done(((bf16[256,288]{0,1:T(8,128)(2,1)}), bf16[2048,288]{0,1:T(8,128)(2,1)}) %all-gather.2.cloned.1.call-update) | async-done | bytes 1179664 | tf_op jit(solution)/shard_map/all_gather | solution.py:66
  36.8 0.0 copy-done
  36.8 3.3 %fusion.5 = f32[256,2048]{1,0:T(8,128)} fusion(bf16[256,288]{0,1:T(8,128)(2,1)S(1)} %copy-done, bf16[2048,288]{0,1:T(8,128)(2,1)} %all-gather.2.cloned.1.call-done), kind=kOutput, calls=%fused_computation.24 | convolution fusion | flops 301989888 | bytes 3424256 | tf_op jit(solution)/shard_map/dot_general | solution.py:16
  40.1 0.0 all-reduce.2.cloned.1.call-update
  40.1 0.0 reduce-scatter.2.cloned.1.call-start
  41.5 0.0 copy-done.2
  41.5 85.3 %all-reduce.2.cloned.1.call-done = f32[256,2048]{1,0:T(8,128)} async-done(((f32[256,2048]{1,0:T(8,128)}), f32[256,2048]{1,0:T(8,128)}) %all-reduce.2.cloned.1.call-update) | async-done | bytes 2097168 | tf_op jit(solution)/shard_map/psum | solution.py:67
  126.8 2.2 %fusion.1 = bf16[256,2048]{1,0:T(8,128)(2,1)S(1)} fusion(f32[256,2048]{1,0:T(8,128)} %all-reduce.2.cloned.1.call-done, s32[2048]{0:T(1024)S(1)} %get-tuple-element.2, s32[2048]{0:T(1024)S(1)} %get-tuple-element.3, s32[]{:T(128)S(6)} %axis_index.15, s32[256]{0:T(256)S(1)} %bitcast.13, f32[]{:T(128)} %bitcast.12, f32[]{:T(128)} %bitcast.10, ...), kind=kLoop, calls=%fused_computation.14 | loop fusion | flops 21495808 | bytes 3165196 | tf_op jit(solution)/shard_map/mul | solution.py:77
  128.9 1.9 %fusion.6 = f32[2048,288]{0,1:T(8,128)} fusion(bf16[256,288]{0,1:T(8,128)(2,1)S(1)} %copy-done, bf16[256,2048]{1,0:T(8,128)(2,1)S(1)} %fusion.1), kind=kOutput, calls=%fused_computation.25 | convolution fusion | flops 301989888 | bytes 3555328 | tf_op jit(solution)/shard_map/dot_general | solution.py:22
  130.8 0.0 copy-start.1
  130.8 0.0 reduce-scatter.2.cloned.1.call-update
  130.8 1.2 copy-done.1
  132.1 1.2 convolution_multiply_fusion
  133.3 39.1 %reduce-scatter.2.cloned.1.call-done = f32[256,288]{0,1:T(8,128)} async-done(((f32[2048,288]{0,1:T(8,128)}), f32[256,288]{0,1:T(8,128)}) %reduce-scatter.2.cloned.1.call-update) | async-done | bytes 294928 | tf_op jit(solution)/shard_map/reduce_scatter | solution.py:79
  172.4 1.7 broadcast_multiply_fusion
  (3 shorter events, 0.0 us)
Async XLA Ops:
  7.2 29.6 %copy-start = (bf16[256,288]{0,1:T(8,128)(2,1)S(1)}, bf16[256,288]{0,1:T(8,128)(2,1)}, u32[]{:S(2)}) copy-start(bf16[256,288]{0,1:T(8,128)(2,1)} %param.5) | copy-start | bytes 442372
  7.2 29.6 %all-gather.2.cloned.1.call-start = ((), (), s32[]{:S(2)}) async-start(), calls=%async_computation.1 | async-start | bytes 1327104 | tf_op jit(solution)/shard_map/all_gather | solution.py:66
  7.9 33.6 %copy-start.2 = (s32[1,256]{1,0:T(1,128)S(1)}, s32[1,256]{1,0:T(1,128)}, u32[]{:S(2)}) copy-start(s32[1,256]{1,0:T(1,128)} %param.7) | copy-start | bytes 3076
  7.9 118.8 %all-reduce.2.cloned.1.call-start = ((), (), s32[]{:S(2)}) async-start(), calls=%async_computation.2 | async-start | bytes 4194304 | tf_op jit(solution)/shard_map/psum | solution.py:67
  40.1 132.3 %reduce-scatter.2.cloned.1.call-start = ((), (), s32[]{:S(2)}) async-start(), calls=%async_computation.3 | async-start | bytes 2654208 | tf_op jit(solution)/shard_map/reduce_scatter | solution.py:79
  130.8 1.3 copy-start.1
Sparse Core Ops, SparseCore 0:
  9.9 26.8 all-gather.1
  40.2 86.4 all-reduce.1
  131.0 41.4 reduce-scatter.1

commit v2 on v0

--- a/solution.py
+++ b/solution.py
@@ -1,9 +1,14 @@
+import functools
+
 import jax
 import jax.numpy as jnp
 from jax import lax
+from jax.experimental import pallas as pl
+from jax.experimental.pallas import tpu as pltpu
 from jax.sharding import PartitionSpec as P
 
 REACH = 7
+MESH = pl.DeviceIdType.MESH
 
 
 def shifted(block, axis, distance):
@@ -24,7 +29,7 @@
     )
 
 
-def per_device(images, texts, matches, scale, shift_bias):
+def band(images, texts, matches, scale, shift_bias):
     temper = scale[0]
     offset_bias = shift_bias[0]
     rows = images.shape[0]
@@ -58,10 +63,181 @@
     return (temper * grad_image, temper * grad_text)
 
 
+def kernel(
+    n, m, images, texts, matches, params, grad_image, grad_text,
+    image_slabs, text_slabs, text_terms, text_got, image_terms, image_got, text_sums, text_final,
+    quarter_send, quarter_recv, image_send, image_recv, plane_send, plane_recv,
+    term_send, term_recv, back_send, back_recv, final_send, final_recv,
+):
+    t, z = lax.axis_index("tour"), lax.axis_index("width")
+    rows, width = images.shape
+    part = rows // m
+    temper, offset_bias = params[0], params[1]
+
+    def along(k):
+        return lax.rem(t + k, n)
+
+    def across(k):
+        return lax.rem(z + k, m)
+
+    def quarter(k):
+        return pl.ds(pl.multiple_of(across(k) * part, part), part)
+
+    def send(src, dst, send_sem, recv_sem, device):
+        copy = pltpu.make_async_remote_copy(
+            src_ref=src, dst_ref=dst, send_sem=send_sem, recv_sem=recv_sem,
+            device_id=device, device_id_type=MESH,
+        )
+        copy.start()
+        return copy
+
+    barrier = pltpu.get_barrier_semaphore()
+    for k in range(1, m):
+        pl.semaphore_signal(barrier, inc=1, device_id={"width": across(k)}, device_id_type=MESH)
+    for k in range(1, n):
+        pl.semaphore_signal(barrier, inc=1, device_id={"tour": along(k)}, device_id_type=MESH)
+    text_slabs[0, 0] = texts[quarter(0), :]
+    pl.semaphore_wait(barrier, n + m - 2)
+
+    sent = []
+    quarters, slabs, plane = {}, {}, {}
+    for k in range(1, m):
+        e = m - k
+        quarters[e] = send(
+            texts.at[quarter(k)], text_slabs.at[0, e], quarter_send.at[e], quarter_recv.at[e],
+            {"width": across(k)},
+        )
+
+    def spread(e):
+        for k in range(1, n):
+            d = n - k
+            plane[d, e] = send(
+                text_slabs.at[0, e], text_slabs.at[d, e], plane_send.at[d, e], plane_recv.at[d, e],
+                {"tour": along(k)},
+            )
+
+    spread(0)
+    for k in range(1, m):
+        e = m - k
+        slabs[e] = send(
+            images, image_slabs.at[e - 1], image_send.at[e], image_recv.at[e], {"width": across(k)}
+        )
+    for e in range(1, m):
+        quarters[e].wait_recv()
+        spread(e)
+
+    def image_slab(e):
+        return images[...] if e == 0 else image_slabs[e - 1]
+
+    def text_slab(e):
+        return text_slabs[:, e].reshape(n * part, width)
+
+    total = None
+    for e in range(m):
+        if e > 0:
+            slabs[e].wait_recv()
+        for d in range(1, n):
+            plane[d, e].wait_recv()
+        term = cross_rows(text_slab(e), image_slab(e))
+        total = term if total is None else total + term
+    probs = jax.nn.sigmoid(temper * total + offset_bias)
+    place = lax.broadcasted_iota(jnp.int32, (part, rows), 0) + z * part
+    label = (place == matches[...]).astype(jnp.float32)
+    pieces = []
+    for d in range(n):
+        count = len([s for s in range(-REACH, REACH + 1) if (s + d) % n == 0])
+        piece = probs[d * part : (d + 1) * part]
+        if d == 0:
+            piece = piece - label
+        pieces.append(piece.astype(jnp.bfloat16).astype(jnp.float32) * count)
+    weights = jnp.concatenate(pieces, axis=0)
+    turned = weights.T.astype(jnp.bfloat16)
+    weights = weights.astype(jnp.bfloat16)
+
+    own = []
+    for e in range(m):
+        term = jnp.dot(weights, image_slab(e), preferred_element_type=jnp.float32)
+        own.append(term[:part])
+        for d in range(1, n):
+            text_terms[d - 1, e] = term[d * part : (d + 1) * part].astype(jnp.bfloat16)
+    terms, backs, finals = {}, {}, {}
+    for d in range(1, n):
+        terms[n - d] = send(
+            text_terms.at[d - 1], text_got.at[n - d - 1], term_send.at[d], term_recv.at[n - d],
+            {"tour": along(d)},
+        )
+    for e in range(1, m):
+        term = jnp.dot(turned, text_slab(e), preferred_element_type=jnp.float32)
+        image_terms[e - 1] = term.astype(jnp.bfloat16)
+        backs[m - e] = send(
+            image_terms.at[e - 1], image_got.at[m - e - 1], back_send.at[e], back_recv.at[m - e],
+            {"width": across(e)},
+        )
+    kept = jnp.dot(turned, text_slab(0), preferred_element_type=jnp.float32)
+
+    for d in range(1, n):
+        terms[d].wait_recv()
+    for e in list(range(1, m)) + [0]:
+        value = own[e]
+        for d in range(1, n):
+            value = value + text_got[d - 1, e].astype(jnp.float32)
+        value = temper * value
+        if e == 0:
+            grad_text[quarter(0), :] = value
+        else:
+            text_sums[e - 1] = value
+            finals[m - e] = send(
+                text_sums.at[e - 1], text_final.at[m - e - 1], final_send.at[e], final_recv.at[m - e],
+                {"width": across(e)},
+            )
+    for e in range(1, m):
+        backs[e].wait_recv()
+        kept = kept + image_got[e - 1].astype(jnp.float32)
+    grad_image[...] = temper * kept
+    for e in range(1, m):
+        finals[e].wait_recv()
+        grad_text[quarter(e), :] = text_final[e - 1]
+    for group in (quarters, slabs, plane, terms, backs, finals):
+        for copy in group.values():
+            copy.wait_send()
+
+
+def whole(images, texts, matches, scale, shift_bias):
+    n, m = lax.axis_size("tour"), lax.axis_size("width")
+    rows, width = images.shape
+    part = rows // m
+    params = jnp.concatenate([scale, shift_bias])
+    vmem = pl.BlockSpec(memory_space=pltpu.VMEM)
+    dma = pltpu.SemaphoreType.DMA
+    out = jax.ShapeDtypeStruct((rows, width), jnp.float32)
+    return pl.pallas_call(
+        functools.partial(kernel, n, m),
+        out_shape=(out, out),
+        in_specs=[vmem, vmem, vmem, pl.BlockSpec(memory_space=pltpu.SMEM)],
+        out_specs=(vmem, vmem),
+        scratch_shapes=[
+            pltpu.VMEM((m - 1, rows, width), jnp.bfloat16),
+            pltpu.VMEM((n, m, part, width), jnp.bfloat16),
+            pltpu.VMEM((n - 1, m, part, width), jnp.bfloat16),
+            pltpu.VMEM((n - 1, m, part, width), jnp.bfloat16),
+            pltpu.VMEM((m - 1, rows, width), jnp.bfloat16),
+            pltpu.VMEM((m - 1, rows, width), jnp.bfloat16),
+            pltpu.VMEM((m - 1, part, width), jnp.float32),
+            pltpu.VMEM((m - 1, part, width), jnp.float32),
+            dma((m,)), dma((m,)), dma((m,)), dma((m,)), dma((n, m)), dma((n, m)),
+            dma((n,)), dma((n,)), dma((m,)), dma((m,)), dma((m,)), dma((m,)),
+        ],
+        compiler_params=pltpu.CompilerParams(
+            collective_id=0, has_side_effects=True, vmem_limit_bytes=48 * 1024 * 1024
+        ),
+    )(images, texts, matches, params)
+
+
 def solution(mesh):
     placed = (P("tour", "width"), P("tour", "width"), P("tour", None), P(), P())
+    body = whole if mesh.shape["tour"] <= 2 * REACH + 1 else band
     return jax.shard_map(
-        per_device,
+        body,
         mesh=mesh,
         in_specs=placed,
         out_specs=(P("tour", "width"), P("tour", "width")),

time: 162 us -> 62.5 us (0.39)
  the two profiles are of different devices: /device:TPU:0 before, /device:TPU:24 now
where the time goes in v2:
time: 62.5 us; the launch traced here: 62.3 us
  Pallas kernels  56.8 us (91%)
  local copies, waits for them, and re-layouts  3.49 us (6%)
  between operations  1.96 us (3%)
    pallas_call x1, Pallas kernels, whole(): pl.pallas_call(functools.partial(kernel, n, m), out_shape=(out, out), in_...  56.8 us
    unnamed x6, local copies, waits for them, and re-layouts  1.78 us
    pallas_call x2, local copies, waits for them, and re-layouts, whole(): pl.pallas_call(functools.partial(kernel, n, m), out_shape=(out, out), in_...  1.71 us

profile of v2, /device:TPU:24, one launch (start us, length us, event | category | flops | bytes accessed | tf_op | source)
XLA Modules:
  0.0 62.3 jit_solution(6921811629217261147)
XLA Ops:
  1.9 0.1 pad_maximum_fusion.params
  2.0 0.0 copy-start.1
  2.0 1.1 %copy.7.images = bf16[256,288]{1,0:T(8,128)(2,1)S(1)} copy(bf16[256,288]{0,1:T(8,128)(2,1)} %param.5) | data formatting | bytes 294912 | tf_op args[0]
  3.1 0.0 copy-done.1
  3.1 0.0 copy-start
  3.1 0.2 copy.8.texts
  3.3 0.5 copy-done
  3.8 56.8 %shard_map.68 = (f32[256,288]{1,0:T(8,128)S(1)}, f32[256,288]{1,0:T(8,128)S(1)}) custom-call(bf16[256,288]{1,0:T(8,128)(2,1)S(1)} %copy.7.images, bf16[256,288]{1,0:T(8,128)(2,1)S(1)} %copy.8.texts, s32[1,256]{1,0:T(1,128)S(1)} %copy-done, f32[2]{0:T(128)S(1)} %pad_maximum_fusion.params), custom_call_target="tpu_custom_call" | custom-call | tf_op jit(solution)/shard_map/pallas_call | solution.py:213
  60.6 0.9 %copy.9 = f32[256,288]{0,1:T(8,128)} copy(f32[256,288]{1,0:T(8,128)S(1)} %get-tuple-element.2) | data formatting | bytes 589824 | tf_op jit(solution)/shard_map/pallas_call | solution.py:213
  61.4 0.9 %copy.10 = f32[256,288]{0,1:T(8,128)} copy(f32[256,288]{1,0:T(8,128)S(1)} %get-tuple-element.3) | data formatting | bytes 589824 | tf_op jit(solution)/shard_map/pallas_call | solution.py:213
Async XLA Ops:
  2.0 1.1 %copy-start.1 = (bf16[256,288]{0,1:T(8,128)(2,1)S(1)}, bf16[256,288]{0,1:T(8,128)(2,1)}, u32[]{:S(2)}) copy-start(bf16[256,288]{0,1:T(8,128)(2,1)} %param.6) | copy-start | bytes 442372
  3.1 0.7 %copy-start = (s32[1,256]{1,0:T(1,128)S(1)}, s32[1,256]{1,0:T(1,128)}, u32[]{:S(2)}) copy-start(s32[1,256]{1,0:T(1,128)} %matches.1) | copy-start | bytes 3076

commit v3 on v0

--- a/solution.py
+++ b/solution.py
@@ -1,9 +1,14 @@
+import functools
+
 import jax
 import jax.numpy as jnp
 from jax import lax
+from jax.experimental import pallas as pl
+from jax.experimental.pallas import tpu as pltpu
 from jax.sharding import PartitionSpec as P
 
 REACH = 7
+MESH = pl.DeviceIdType.MESH
 
 
 def shifted(block, axis, distance):
@@ -24,7 +29,7 @@
     )
 
 
-def per_device(images, texts, matches, scale, shift_bias):
+def band(images, texts, matches, scale, shift_bias):
     temper = scale[0]
     offset_bias = shift_bias[0]
     rows = images.shape[0]
@@ -58,10 +63,266 @@
     return (temper * grad_image, temper * grad_text)
 
 
+def kernel(
+    n, m, images, texts, matches, params, grad_image, grad_text,
+    image_all, text_all, text_terms, term_got, text_got, text_own, text_sums, text_final,
+    image_terms, image_got,
+    quarter_send, quarter_recv, image_send, image_recv, plane_send, plane_recv, share_send,
+    term_send, term_recv, hop_send, hop_recv, back_send, back_recv, final_send, final_recv,
+):
+    t, z = lax.axis_index("tour"), lax.axis_index("width")
+    width, rows = images.shape
+    cores = 2
+    halves, chips = m // cores, n // cores
+    half = rows // halves
+    temper, offset_bias = params[0], params[1]
+    core, chip = lax.rem(t, cores), lax.div(t, cores)
+    plane_core, plane_half = lax.div(z, halves), lax.rem(z, halves)
+    keeper = core == plane_core
+    helper = core != plane_core
+    sibling = chip * cores + (cores - 1 - core)
+    slabs = [lax.rem(z + k, m) for k in range(m)]
+    keepers = [lax.rem(chip + r, chips) * cores + plane_core for r in range(chips)]
+    targets = [core * halves + h for h in range(halves)]
+    elsewhere = [target != z for target in targets]
+    everyone = z >= 0
+    started = []
+
+    def remote(src, dst, send_sem, recv_sem, device):
+        return pltpu.make_async_remote_copy(
+            src_ref=src, dst_ref=dst, send_sem=send_sem, recv_sem=recv_sem,
+            device_id=device, device_id_type=MESH,
+        )
+
+    def arriving(dst, recv_sem):
+        return remote(dst, dst, quarter_send.at[0], recv_sem, {"width": slabs[1]})
+
+    quarter = [
+        remote(
+            texts.at[:, h * half : (h + 1) * half], text_all.at[0, z],
+            quarter_send.at[h], quarter_recv.at[z], {"width": targets[h]},
+        )
+        for h in range(halves)
+    ]
+    image, image_in, quarter_in, back, back_in, final = {}, {}, {}, {}, {}, {}
+    plane, plane_in, share, term_out, hop, hop_in = {}, {}, {}, {}, {}, {}
+    for k in range(1, m):
+        f = slabs[k]
+        quarter_in[k] = arriving(text_all.at[0, f], quarter_recv.at[f])
+        image[k] = remote(images, image_all.at[z], image_send.at[k], image_recv.at[z], {"width": f})
+        image_in[k] = arriving(image_all.at[f], image_recv.at[f])
+        back[k] = remote(
+            image_terms.at[k - 1], image_got.at[z], back_send.at[k], back_recv.at[z], {"width": f}
+        )
+        back_in[k] = arriving(image_got.at[f], back_recv.at[f])
+        final[k] = remote(
+            text_sums.at[k - 1], text_final.at[plane_half],
+            final_send.at[k], final_recv.at[plane_half], {"width": f},
+        )
+    final_in = [arriving(text_final.at[h], final_recv.at[h]) for h in range(halves)]
+    for r in range(chips):
+        for k in range(m):
+            f = slabs[k]
+            plane_in[r, k] = arriving(text_all.at[r, f], plane_recv.at[r, f])
+            share[r, k] = remote(
+                text_all.at[r, f], text_all.at[r, f], share_send.at[r, k], plane_recv.at[r, f],
+                {"tour": sibling},
+            )
+            if r > 0:
+                plane[r, k] = remote(
+                    text_all.at[0, f], text_all.at[chips - r, f],
+                    plane_send.at[r, k], plane_recv.at[chips - r, f], {"tour": keepers[r]},
+                )
+        term_out[r] = remote(
+            text_terms.at[r], term_got.at[r], term_send.at[r], term_recv.at[r], {"tour": sibling}
+        )
+        if r > 0:
+            hop[r] = remote(
+                text_terms.at[r], text_got.at[chips - r - 1],
+                hop_send.at[r], hop_recv.at[chips - r], {"tour": keepers[r]},
+            )
+            hop_in[r] = arriving(text_got.at[r - 1], hop_recv.at[r])
+
+    barrier = pltpu.get_barrier_semaphore()
+    for k in range(1, m):
+        pl.semaphore_signal(barrier, inc=1, device_id={"width": slabs[k]}, device_id_type=MESH)
+    for k in range(1, n):
+        pl.semaphore_signal(
+            barrier, inc=1, device_id={"tour": lax.rem(t + k, n)}, device_id_type=MESH
+        )
+    image_all[z] = images[...]
+    for h in range(halves):
+        @pl.when(targets[h] == z)
+        def _():
+            text_all[0, z] = texts[:, h * half : (h + 1) * half]
+    spot = jnp.broadcast_to(matches[...].astype(jnp.float32), (half, rows)).T
+    pl.semaphore_wait(barrier, n + m - 2)
+
+    for h in range(halves):
+        @pl.when(elsewhere[h])
+        def _():
+            quarter[h].start()
+    for k in (2, 1, 3):
+        image[k].start()
+
+    @pl.when(keeper)
+    def _():
+        for k in range(m):
+            if k > 0:
+                quarter_in[k].wait_recv()
+            for r in range(1, chips):
+                plane[r, k].start()
+            share[0, k].start()
+        for k in range(m):
+            for r in range(1, chips):
+                plane_in[r, k].wait_recv()
+                share[r, k].start()
+
+    @pl.when(helper)
+    def _():
+        for k in range(m):
+            for r in range(chips):
+                plane_in[r, k].wait_recv()
+
+    def text_slab(f):
+        return jnp.concatenate([text_all[r, f] for r in range(chips)], axis=1)
+
+    total = None
+    for k in range(m):
+        if k > 0:
+            image_in[k].wait_recv()
+        term = cross_cols(image_all[slabs[k]], text_slab(slabs[k]))
+        total = term if total is None else total + term
+    probs = jax.nn.sigmoid(temper * total + offset_bias)
+    column = lax.broadcasted_iota(jnp.int32, (rows, half), 1) + plane_half * half
+    hit = jnp.where(keeper, 1.0, 0.0) * (column.astype(jnp.float32) == spot).astype(jnp.float32)
+    counts = [len([s for s in range(-REACH, REACH + 1) if s % n == d]) for d in range(n)]
+    weights, turned = [], []
+    for r in range(chips):
+        piece = probs[:, r * half : (r + 1) * half]
+        if r == 0:
+            piece = piece - hit
+        distance = lax.rem(t - keepers[r] + n, n)
+        count = jnp.float32(0)
+        for d in range(n):
+            count = jnp.where(distance == d, jnp.float32(counts[d]), count)
+        piece = piece.astype(jnp.bfloat16).astype(jnp.float32) * count
+        weights.append(piece.astype(jnp.bfloat16))
+        turned.append(piece.T.astype(jnp.bfloat16))
+    turned = jnp.concatenate(turned, axis=0)
+
+    image_rows = image_all[...].reshape(m * width, rows)
+    for r in list(range(1, chips)) + [0]:
+        term = jnp.dot(image_rows, weights[r], preferred_element_type=jnp.float32)
+
+        @pl.when(helper)
+        def _():
+            text_terms[r] = term.astype(jnp.bfloat16)
+            term_out[r].start()
+
+        @pl.when(keeper)
+        def _():
+            term_out[r].wait_recv()
+            both = term + term_got[r].astype(jnp.float32)
+            if r == 0:
+                text_own[...] = both
+            else:
+                text_terms[r] = both.astype(jnp.bfloat16)
+                hop[r].start()
+
+    for k in (2, 1, 3, 0):
+        term = jnp.dot(text_slab(slabs[k]), turned, preferred_element_type=jnp.float32)
+        if k == 0:
+            kept = term
+        else:
+            image_terms[k - 1] = term.astype(jnp.bfloat16)
+            back[k].start()
+
+    @pl.when(keeper)
+    def _():
+        for r in range(1, chips):
+            hop_in[r].wait_recv()
+        for k in (2, 1, 3, 0):
+            span = pl.ds(pl.multiple_of(slabs[k] * width, width), width)
+            value = text_own[span, :]
+            for r in range(1, chips):
+                value = value + text_got[r - 1, span, :].astype(jnp.float32)
+            value = temper * value
+            if k == 0:
+                text_final[plane_half] = value
+            else:
+                text_sums[k - 1] = value
+                final[k].start()
+
+    for k in range(1, m):
+        back_in[k].wait_recv()
+        kept = kept + image_got[slabs[k]].astype(jnp.float32)
+    grad_image[...] = temper * kept
+    for h in range(halves):
+        @pl.when(elsewhere[h])
+        def _():
+            final_in[h].wait_recv()
+            quarter[h].wait_send()
+        grad_text[:, h * half : (h + 1) * half] = text_final[h]
+    for group in (image, back):
+        for copy in group.values():
+            copy.wait_send()
+
+    @pl.when(keeper)
+    def _():
+        for group in (plane, share, hop, final):
+            for copy in group.values():
+                copy.wait_send()
+
+    @pl.when(helper)
+    def _():
+        for copy in term_out.values():
+            copy.wait_send()
+
+
+def whole(images, texts, matches, scale, shift_bias):
+    n, m = lax.axis_size("tour"), lax.axis_size("width")
+    rows, width = images.shape
+    chips, half, full = n // 2, rows // (m // 2), m * width
+    params = jnp.concatenate([scale, shift_bias])
+    vmem = pl.BlockSpec(memory_space=pltpu.VMEM)
+    out = jax.ShapeDtypeStruct((width, rows), jnp.float32)
+
+    def dma(*shape):
+        return pltpu.SemaphoreType.DMA(shape)
+
+    grads = pl.pallas_call(
+        functools.partial(kernel, n, m),
+        out_shape=(out, out),
+        in_specs=[vmem, vmem, vmem, pl.BlockSpec(memory_space=pltpu.SMEM)],
+        out_specs=(vmem, vmem),
+        scratch_shapes=[
+            pltpu.VMEM((m, width, rows), jnp.bfloat16),
+            pltpu.VMEM((chips, m, width, half), jnp.bfloat16),
+            pltpu.VMEM((chips, full, half), jnp.bfloat16),
+            pltpu.VMEM((chips, full, half), jnp.bfloat16),
+            pltpu.VMEM((chips - 1, full, half), jnp.bfloat16),
+            pltpu.VMEM((full, half), jnp.float32),
+            pltpu.VMEM((m - 1, width, half), jnp.float32),
+            pltpu.VMEM((m // 2, width, half), jnp.float32),
+            pltpu.VMEM((m - 1, width, rows), jnp.bfloat16),
+            pltpu.VMEM((m, width, rows), jnp.bfloat16),
+            dma(m), dma(m), dma(m), dma(m), dma(chips, m), dma(chips, m), dma(chips, m),
+            dma(chips), dma(chips), dma(chips), dma(chips), dma(m), dma(m), dma(m), dma(m),
+        ],
+        compiler_params=pltpu.CompilerParams(
+            collective_id=0, has_side_effects=True, vmem_limit_bytes=48 * 1024 * 1024
+        ),
+    )(images.T, texts.T, matches, params)
+    return tuple(grad.T for grad in grads)
+
+
 def solution(mesh):
     placed = (P("tour", "width"), P("tour", "width"), P("tour", None), P(), P())
+    n, m = mesh.shape["tour"], mesh.shape["width"]
+    body = whole if n <= 2 * REACH + 1 and n % 2 == 0 and m == 4 else band
     return jax.shard_map(
-        per_device,
+        body,
         mesh=mesh,
         in_specs=placed,
         out_specs=(P("tour", "width"), P("tour", "width")),

time: 162 us -> 54.3 us (0.34)
  the two profiles are of different devices: /device:TPU:0 before, /device:TPU:16 now
where the time goes in v3:
time: 54.3 us; the launch traced here: 54.1 us
  Pallas kernels  48.2 us (89%)
  local copies, waits for them, and re-layouts  3.93 us (7%)
  between operations  1.93 us (4%)
    pallas_call x1, Pallas kernels, whole(): pl.pallas_call(functools.partial(kernel, n, m), out_shape=(out, out), in_...  48.2 us
    unnamed x8, local copies, waits for them, and re-layouts  3.93 us

profile of v3, /device:TPU:16, one launch (start us, length us, event | category | flops | bytes accessed | tf_op | source)
XLA Modules:
  0.0 54.1 jit_solution(10769021130643985435)
XLA Ops:
  1.9 0.1 pad_maximum_fusion.params
  2.0 0.0 copy-start.2
  2.0 0.7 %copy-done.2 = s32[1,256]{1,0:T(1,128)S(1)} copy-done((s32[1,256]{1,0:T(1,128)S(1)}, s32[1,256]{1,0:T(1,128)}, u32[]{:S(2)}) %copy-start.2) | copy-done | bytes 1048
  2.7 0.0 copy-start
  2.7 0.9 %copy-done = bf16[256,288]{0,1:T(8,128)(2,1)S(1)} copy-done((bf16[256,288]{0,1:T(8,128)(2,1)S(1)}, bf16[256,288]{0,1:T(8,128)(2,1)}, u32[]{:S(2)}) %copy-start) | copy-done | bytes 147480
  3.6 0.0 copy-start.1
  3.6 0.9 %copy-done.1 = bf16[256,288]{0,1:T(8,128)(2,1)S(1)} copy-done((bf16[256,288]{0,1:T(8,128)(2,1)S(1)}, bf16[256,288]{0,1:T(8,128)(2,1)}, u32[]{:S(2)}) %copy-start.1) | copy-done | bytes 147480
  4.5 48.2 %shard_map.68 = (f32[288,256]{1,0:T(8,128)S(1)}, f32[288,256]{1,0:T(8,128)S(1)}) custom-call(bf16[288,256]{1,0:T(8,128)(2,1)S(1)} %bitcast.6, bf16[288,256]{1,0:T(8,128)(2,1)S(1)} %bitcast.7, s32[1,256]{1,0:T(1,128)S(1)} %copy-done.2, f32[2]{0:T(128)S(1)} %pad_maximum_fusion.params), custom_call_target="tpu_custom_call" | custom-call | tf_op jit(solution)/shard_map/pallas_call | solution.py:294
  52.7 0.7 %copy.11 = f32[256,288]{0,1:T(8,128)} copy(f32[256,288]{0,1:T(8,128)S(1)} %bitcast.5) | data formatting | bytes 589824
  53.4 0.7 %copy.12 = f32[256,288]{0,1:T(8,128)} copy(f32[256,288]{0,1:T(8,128)S(1)} %bitcast.4) | data formatting | bytes 589824
Async XLA Ops:
  2.0 0.7 %copy-start.2 = (s32[1,256]{1,0:T(1,128)S(1)}, s32[1,256]{1,0:T(1,128)}, u32[]{:S(2)}) copy-start(s32[1,256]{1,0:T(1,128)} %matches.1) | copy-start | bytes 3076
  2.7 0.9 %copy-start = (bf16[256,288]{0,1:T(8,128)(2,1)S(1)}, bf16[256,288]{0,1:T(8,128)(2,1)}, u32[]{:S(2)}) copy-start(bf16[256,288]{0,1:T(8,128)(2,1)} %param.5) | copy-start | bytes 442372
  3.6 0.9 %copy-start.1 = (bf16[256,288]{0,1:T(8,128)(2,1)S(1)}, bf16[256,288]{0,1:T(8,128)(2,1)}, u32[]{:S(2)}) copy-start(bf16[256,288]{0,1:T(8,128)(2,1)} %param.6) | copy-start | bytes 442372

commit v4 on v3

--- a/solution.py
+++ b/solution.py
@@ -64,14 +64,14 @@
 
 
 def kernel(
-    n, m, images, texts, matches, params, grad_image, grad_text,
-    image_all, text_all, text_terms, term_got, text_got, text_own, text_sums, text_final,
-    image_terms, image_got,
-    quarter_send, quarter_recv, image_send, image_recv, plane_send, plane_recv, share_send,
+    n, m, images_in, texts_in, matches_in, params, grad_image, grad_text,
+    texts, matches, image_all, text_all, text_terms, term_got, text_got, text_own, text_sums, text_final,
+    image_terms, image_sums, image_got,
+    load_sem, relay_send, quarter_send, quarter_recv, image_send, image_recv, plane_send, plane_recv, share_send,
     term_send, term_recv, hop_send, hop_recv, back_send, back_recv, final_send, final_recv,
 ):
     t, z = lax.axis_index("tour"), lax.axis_index("width")
-    width, rows = images.shape
+    width, rows = texts.shape
     cores = 2
     halves, chips = m // cores, n // cores
     half = rows // halves
@@ -85,8 +85,21 @@
     keepers = [lax.rem(chip + r, chips) * cores + plane_core for r in range(chips)]
     targets = [core * halves + h for h in range(halves)]
     elsewhere = [target != z for target in targets]
-    everyone = z >= 0
-    started = []
+    outer = jnp.logical_or(z == 0, z == m - 1)
+    inner = jnp.logical_not(outer)
+    low = z < halves
+    partner = jnp.where(low, 1 - z, 2 * m - 3 - z)
+    far_inner = jnp.where(low, halves, halves - 1)
+    far_outer = jnp.where(low, m - 1, 0)
+    direct = [jnp.logical_or(inner, f != far_outer) for f in slabs]
+
+    loads = [
+        pltpu.make_async_copy(images_in, image_all.at[z], load_sem.at[0]),
+        pltpu.make_async_copy(texts_in, texts, load_sem.at[1]),
+        pltpu.make_async_copy(matches_in, matches, load_sem.at[2]),
+    ]
+    for load in loads:
+        load.start()
 
     def remote(src, dst, send_sem, recv_sem, device):
         return pltpu.make_async_remote_copy(
@@ -104,21 +117,32 @@
         )
         for h in range(halves)
     ]
-    image, image_in, quarter_in, back, back_in, final = {}, {}, {}, {}, {}, {}
+    image, image_in, quarter_in, final = {}, {}, {}, {}
     plane, plane_in, share, term_out, hop, hop_in = {}, {}, {}, {}, {}, {}
     for k in range(1, m):
         f = slabs[k]
         quarter_in[k] = arriving(text_all.at[0, f], quarter_recv.at[f])
-        image[k] = remote(images, image_all.at[z], image_send.at[k], image_recv.at[z], {"width": f})
+        image[k] = remote(image_all.at[z], image_all.at[z], image_send.at[k], image_recv.at[z], {"width": f})
         image_in[k] = arriving(image_all.at[f], image_recv.at[f])
-        back[k] = remote(
-            image_terms.at[k - 1], image_got.at[z], back_send.at[k], back_recv.at[z], {"width": f}
-        )
-        back_in[k] = arriving(image_got.at[f], back_recv.at[f])
         final[k] = remote(
             text_sums.at[k - 1], text_final.at[plane_half],
             final_send.at[k], final_recv.at[plane_half], {"width": f},
         )
+    relay = remote(
+        image_all.at[far_outer], image_all.at[far_outer], relay_send.at[0], image_recv.at[far_outer],
+        {"width": partner},
+    )
+
+    def back(i, slot, device):
+        return remote(
+            image_terms.at[i], image_got.at[slot], back_send.at[i], back_recv.at[slot],
+            {"width": device},
+        )
+
+    near_out = back(2, 2, partner)
+    outer_out = [back(0, 0, partner), back(1, 1, partner)]
+    inner_out = [back(0, 3, far_outer), back(1, 3, far_inner)]
+    back_in = [arriving(image_got.at[i], back_recv.at[i]) for i in range(4)]
     final_in = [arriving(text_final.at[h], final_recv.at[h]) for h in range(halves)]
     for r in range(chips):
         for k in range(m):
@@ -150,12 +174,12 @@
         pl.semaphore_signal(
             barrier, inc=1, device_id={"tour": lax.rem(t + k, n)}, device_id_type=MESH
         )
-    image_all[z] = images[...]
+    for load in loads:
+        load.wait()
     for h in range(halves):
         @pl.when(targets[h] == z)
         def _():
             text_all[0, z] = texts[:, h * half : (h + 1) * half]
-    spot = jnp.broadcast_to(matches[...].astype(jnp.float32), (half, rows)).T
     pl.semaphore_wait(barrier, n + m - 2)
 
     for h in range(halves):
@@ -163,7 +187,10 @@
         def _():
             quarter[h].start()
     for k in (2, 1, 3):
-        image[k].start()
+        @pl.when(direct[k])
+        def _():
+            image[k].start()
+    spot = jnp.broadcast_to(matches[...].astype(jnp.float32), (half, rows)).T
 
     @pl.when(keeper)
     def _():
@@ -173,6 +200,14 @@
             for r in range(1, chips):
                 plane[r, k].start()
             share[0, k].start()
+
+    @pl.when(inner)
+    def _():
+        image_in[2].wait_recv()
+        relay.start()
+
+    @pl.when(keeper)
+    def _():
         for k in range(m):
             for r in range(1, chips):
                 plane_in[r, k].wait_recv()
@@ -189,7 +224,11 @@
 
     total = None
     for k in range(m):
-        if k > 0:
+        if k == 2:
+            @pl.when(outer)
+            def _():
+                image_in[2].wait_recv()
+        elif k > 0:
             image_in[k].wait_recv()
         term = cross_cols(image_all[slabs[k]], text_slab(slabs[k]))
         total = term if total is None else total + term
@@ -211,6 +250,25 @@
         turned.append(piece.T.astype(jnp.bfloat16))
     turned = jnp.concatenate(turned, axis=0)
 
+    def image_term(f):
+        return jnp.dot(text_slab(f), turned, preferred_element_type=jnp.float32)
+
+    for i, f in enumerate((far_outer, far_inner)):
+        term = image_term(f)
+
+        @pl.when(outer)
+        def _():
+            image_terms[i] = term.astype(jnp.bfloat16)
+            outer_out[i].start()
+
+        @pl.when(inner)
+        def _():
+            image_sums[i] = term
+
+    image_terms[2] = image_term(partner).astype(jnp.bfloat16)
+    near_out.start()
+    kept = image_term(z)
+
     image_rows = image_all[...].reshape(m * width, rows)
     for r in list(range(1, chips)) + [0]:
         term = jnp.dot(image_rows, weights[r], preferred_element_type=jnp.float32)
@@ -230,13 +288,13 @@
                 text_terms[r] = both.astype(jnp.bfloat16)
                 hop[r].start()
 
-    for k in (2, 1, 3, 0):
-        term = jnp.dot(text_slab(slabs[k]), turned, preferred_element_type=jnp.float32)
-        if k == 0:
-            kept = term
-        else:
-            image_terms[k - 1] = term.astype(jnp.bfloat16)
-            back[k].start()
+    @pl.when(inner)
+    def _():
+        for i in range(2):
+            back_in[i].wait_recv()
+            value = image_sums[i] + image_got[i].astype(jnp.float32)
+            image_terms[i] = value.astype(jnp.bfloat16)
+            inner_out[i].start()
 
     @pl.when(keeper)
     def _():
@@ -254,9 +312,9 @@
                 text_sums[k - 1] = value
                 final[k].start()
 
-    for k in range(1, m):
-        back_in[k].wait_recv()
-        kept = kept + image_got[slabs[k]].astype(jnp.float32)
+    for i in (2, 3):
+        back_in[i].wait_recv()
+        kept = kept + image_got[i].astype(jnp.float32)
     grad_image[...] = temper * kept
     for h in range(halves):
         @pl.when(elsewhere[h])
@@ -264,8 +322,20 @@
             final_in[h].wait_recv()
             quarter[h].wait_send()
         grad_text[:, h * half : (h + 1) * half] = text_final[h]
-    for group in (image, back):
-        for copy in group.values():
+    for k in range(1, m):
+        @pl.when(direct[k])
+        def _():
+            image[k].wait_send()
+    near_out.wait_send()
+
+    @pl.when(outer)
+    def _():
+        for copy in outer_out:
+            copy.wait_send()
+
+    @pl.when(inner)
+    def _():
+        for copy in [relay] + inner_out:
             copy.wait_send()
 
     @pl.when(keeper)
@@ -285,6 +355,7 @@
     rows, width = images.shape
     chips, half, full = n // 2, rows // (m // 2), m * width
     params = jnp.concatenate([scale, shift_bias])
+    hbm = pl.BlockSpec(memory_space=pltpu.HBM)
     vmem = pl.BlockSpec(memory_space=pltpu.VMEM)
     out = jax.ShapeDtypeStruct((width, rows), jnp.float32)
 
@@ -294,9 +365,11 @@
     grads = pl.pallas_call(
         functools.partial(kernel, n, m),
         out_shape=(out, out),
-        in_specs=[vmem, vmem, vmem, pl.BlockSpec(memory_space=pltpu.SMEM)],
+        in_specs=[hbm, hbm, hbm, pl.BlockSpec(memory_space=pltpu.SMEM)],
         out_specs=(vmem, vmem),
         scratch_shapes=[
+            pltpu.VMEM((width, rows), jnp.bfloat16),
+            pltpu.VMEM((1, rows), jnp.int32),
             pltpu.VMEM((m, width, rows), jnp.bfloat16),
             pltpu.VMEM((chips, m, width, half), jnp.bfloat16),
             pltpu.VMEM((chips, full, half), jnp.bfloat16),
@@ -305,13 +378,14 @@
             pltpu.VMEM((full, half), jnp.float32),
             pltpu.VMEM((m - 1, width, half), jnp.float32),
             pltpu.VMEM((m // 2, width, half), jnp.float32),
-            pltpu.VMEM((m - 1, width, rows), jnp.bfloat16),
-            pltpu.VMEM((m, width, rows), jnp.bfloat16),
-            dma(m), dma(m), dma(m), dma(m), dma(chips, m), dma(chips, m), dma(chips, m),
+            pltpu.VMEM((3, width, rows), jnp.bfloat16),
+            pltpu.VMEM((2, width, rows), jnp.float32),
+            pltpu.VMEM((4, width, rows), jnp.bfloat16),
+            dma(3), dma(1), dma(m), dma(m), dma(m), dma(m), dma(chips, m), dma(chips, m), dma(chips, m),
             dma(chips), dma(chips), dma(chips), dma(chips), dma(m), dma(m), dma(m), dma(m),
         ],
         compiler_params=pltpu.CompilerParams(
-            collective_id=0, has_side_effects=True, vmem_limit_bytes=48 * 1024 * 1024
+            collective_id=0, has_side_effects=True, vmem_limit_bytes=60 * 1024 * 1024
         ),
     )(images.T, texts.T, matches, params)
     return tuple(grad.T for grad in grads)

time: 54.3 us -> 49.7 us (0.915)
  the two profiles are of different devices: /device:TPU:16 before, /device:TPU:0 now
where the time goes in v4:
time: 49.7 us; the launch traced here: 49 us
  Pallas kernels  44 us (89%)
  local copies, waits for them, and re-layouts  2.46 us (5%)
  between operations  1.94 us (4%)
  other arithmetic  0.59 us (1%)
    pallas_call x1, Pallas kernels, whole(): pl.pallas_call(functools.partial(kernel, n, m), out_shape=(out, out), in_...  44 us
    unnamed x4, local copies, waits for them, and re-layouts  2.46 us

profile of v4, /device:TPU:0, one launch (start us, length us, event | category | flops | bytes accessed | tf_op | source)
XLA Modules:
  0.0 49.0 jit_solution(991849649769078959)
XLA Ops:
  1.9 0.6 %pad_maximum_fusion.params = f32[2]{0:T(128)} fusion(f32[1]{0:T(128)S(6)} %copy.10, f32[1]{0:T(128)S(6)} %copy.9), kind=kLoop, calls=%fused_computation | loop fusion | flops 2 | bytes 16 | tf_op jit(solution)/shard_map/concatenate | solution.py:357
  2.5 44.0 %shard_map.68 = (f32[288,256]{1,0:T(8,128)}, f32[288,256]{1,0:T(8,128)}) custom-call(bf16[288,256]{1,0:T(8,128)(2,1)} %bitcast.6, bf16[288,256]{1,0:T(8,128)(2,1)} %bitcast.7, s32[1,256]{1,0:T(1,128)} %matches_in.1, f32[2]{0:T(128)} %pad_maximum_fusion.params), custom_call_target="tpu_custom_call" | custom-call | tf_op jit(solution)/shard_map/pallas_call | solution.py:365
  46.5 0.0 copy-start
  46.5 1.7 %copy.11 = f32[256,288]{0,1:T(8,128)} copy(f32[256,288]{0,1:T(8,128)} %bitcast.5) | data formatting | bytes 589824
  48.3 0.0 copy-done
  48.3 0.7 %copy.12 = f32[256,288]{0,1:T(8,128)} copy(f32[256,288]{0,1:T(8,128)S(1)} %bitcast.4) | data formatting | bytes 589824
Async XLA Ops:
  46.5 1.8 %copy-start = (f32[288,256]{1,0:T(8,128)S(1)}, f32[288,256]{1,0:T(8,128)}, u32[]{:S(2)}) copy-start(f32[288,256]{1,0:T(8,128)} %get-tuple-element.5) | copy-start | bytes 884740

commit v5 on v3

v5 whole, which is shorter than its diff:
```python
import functools

import jax
import jax.numpy as jnp
from jax import lax
from jax.experimental import pallas as pl
from jax.experimental.pallas import tpu as pltpu
from jax.sharding import PartitionSpec as P

REACH = 7
MESH = pl.DeviceIdType.MESH


def shifted(block, axis, distance):
    devices = range(lax.axis_size(axis))
    route = [((i - distance) % len(devices), i) for i in devices]
    return lax.ppermute(block, axis, route)


def cross_rows(left, right):
    return lax.dot_general(
        left, right, (((1,), (1,)), ((), ())), preferred_element_type=jnp.float32
    )


def cross_cols(weights, right):
    return lax.dot_general(
        weights, right, (((0,), (0,)), ((), ())), preferred_element_type=jnp.float32
    )


def band(images, texts, matches, scale, shift_bias):
    temper = scale[0]
    offset_bias = shift_bias[0]
    rows = images.shape[0]
    columns = lax.broadcasted_iota(jnp.int32, (rows, rows), 1)
    positive = (columns == matches[0][:, None]).astype(jnp.float32)

    def to_weights(total, label):
        probs = jax.nn.sigmoid(temper * total + offset_bias)
        if label is not None:
            probs = probs - label
        return probs.astype(jnp.bfloat16)

    def finish(parts, labels):
        totals = lax.psum(parts, "width")
        return tuple((to_weights(total, label) for total, label in zip(totals, labels)))

    own = finish((cross_rows(images, texts),), (positive,))[0]
    grad_image = jnp.dot(own, texts, preferred_element_type=jnp.float32)
    grad_text = cross_cols(own, images)
    for step in range(1, REACH + 1):
        lower = shifted(texts, "tour", step)
        upper = shifted(texts, "tour", -step)
        weight_low, weight_up = finish(
            (cross_rows(images, lower), cross_rows(images, upper)), (None, None)
        )
        grad_image = grad_image + jnp.dot(weight_low, lower, preferred_element_type=jnp.float32)
        grad_image = grad_image + jnp.dot(weight_up, upper, preferred_element_type=jnp.float32)
        back_low = shifted(cross_cols(weight_low, images), "tour", -step)
        back_up = shifted(cross_cols(weight_up, images), "tour", step)
        grad_text = grad_text + back_low + back_up
    return (temper * grad_image, temper * grad_text)


def kernel(
    n, m, images_in, texts_in, matches_in, scale, shift_bias, grad_image, grad_text,
    texts, matches, image_all, text_all, text_terms, term_got, text_got, text_own, text_sums, text_final,
    image_terms, image_sums, image_got, image_final,
    load_sem, store_sem, relay_send, quarter_send, quarter_recv, image_send, image_recv,
    plane_send, plane_recv, share_send, term_send, term_recv, hop_send, hop_recv,
    back_send, back_recv, final_send, final_recv,
):
    t, z = lax.axis_index("tour"), lax.axis_index("width")
    width, rows = texts.shape
    cores = 2
    halves, chips = m // cores, n // cores
    half = rows // halves
    temper, offset_bias = scale[0], shift_bias[0]
    core, chip = lax.rem(t, cores), lax.div(t, cores)
    plane_core, plane_half = lax.div(z, halves), lax.rem(z, halves)
    keeper = core == plane_core
    helper = core != plane_core
    sibling = chip * cores + (cores - 1 - core)
    slabs = [lax.rem(z + k, m) for k in range(m)]
    keepers = [lax.rem(chip + r, chips) * cores + plane_core for r in range(chips)]
    targets = [core * halves + h for h in range(halves)]
    elsewhere = [target != z for target in targets]
    both_halves = range(halves)
    spans = [slice(p * half, (p + 1) * half) for p in both_halves]
    outer = jnp.logical_or(z == 0, z == m - 1)
    inner = jnp.logical_not(outer)
    low = z < halves
    partner = jnp.where(low, 1 - z, 2 * m - 3 - z)
    far_inner = jnp.where(low, halves, halves - 1)
    far_outer = jnp.where(low, m - 1, 0)
    direct = [jnp.logical_or(inner, f != far_outer) for f in slabs]
    order = (far_outer, far_inner, partner, z)

    loads = [
        pltpu.make_async_copy(images_in, image_all.at[z], load_sem.at[0]),
        pltpu.make_async_copy(texts_in, texts, load_sem.at[1]),
        pltpu.make_async_copy(matches_in, matches, load_sem.at[2]),
    ]
    for load in loads:
        load.start()

    def remote(src, dst, send_sem, recv_sem, device):
        return pltpu.make_async_remote_copy(
            src_ref=src, dst_ref=dst, send_sem=send_sem, recv_sem=recv_sem,
            device_id=device, device_id_type=MESH,
        )

    def arriving(dst, recv_sem):
        return remote(dst, dst, quarter_send.at[0], recv_sem, {"width": slabs[1]})

    quarter = [
        remote(
            texts.at[:, spans[h]], text_all.at[0, z],
            quarter_send.at[h], quarter_recv.at[z], {"width": targets[h]},
        )
        for h in both_halves
    ]
    image, image_in, quarter_in, final = {}, {}, {}, {}
    plane, plane_in, share, term_out, hop, hop_in = {}, {}, {}, {}, {}, {}
    for k in range(1, m):
        f = slabs[k]
        quarter_in[k] = arriving(text_all.at[0, f], quarter_recv.at[f])
        for p in both_halves:
            mine, theirs = image_all.at[z, :, spans[p]], image_all.at[f, :, spans[p]]
            image[p, k] = remote(
                mine, mine, image_send.at[p, k], image_recv.at[p, z], {"width": f}
            )
            image_in[p, k] = arriving(theirs, image_recv.at[p, f])
    relay, near_out, outer_out, inner_out, back_in = [], [], [], [], []
    for p in both_halves:
        passed = image_all.at[far_outer, :, spans[p]]
        relay.append(
            remote(
                passed, passed, relay_send.at[p], image_recv.at[p, far_outer], {"width": partner}
            )
        )

        def back(i, slot, device):
            return remote(
                image_terms.at[p, i], image_got.at[p, slot],
                back_send.at[p, i], back_recv.at[p, slot], {"width": device},
            )

        near_out.append(back(2, 2, partner))
        outer_out.append([back(0, 0, partner), back(1, 1, partner)])
        inner_out.append([back(0, 3, far_outer), back(1, 3, far_inner)])
        back_in.append([arriving(image_got.at[p, i], back_recv.at[p, i]) for i in range(4)])
    final_in = [arriving(text_final.at[h], final_recv.at[h]) for h in both_halves]
    for r in range(chips):
        for k in range(m):
            f = slabs[k]
            plane_in[r, k] = arriving(text_all.at[r, f], plane_recv.at[r, f])
            share[r, k] = remote(
                text_all.at[r, f], text_all.at[r, f], share_send.at[r, k], plane_recv.at[r, f],
                {"tour": sibling},
            )
            if r > 0:
                plane[r, k] = remote(
                    text_all.at[0, f], text_all.at[chips - r, f],
                    plane_send.at[r, k], plane_recv.at[chips - r, f], {"tour": keepers[r]},
                )
    for i in range(m):
        term_out[i] = remote(
            text_terms.at[i], term_got.at[i], term_send.at[i], term_recv.at[i], {"tour": sibling}
        )
        for r in range(1, chips):
            hop[i, r] = remote(
                text_terms.at[i, r], text_got.at[i, chips - r - 1],
                hop_send.at[i, r], hop_recv.at[i, chips - r], {"tour": keepers[r]},
            )
            hop_in[i, r] = arriving(text_got.at[i, r - 1], hop_recv.at[i, r])
        if i < m - 1:
            final[i] = remote(
                text_sums.at[i], text_final.at[plane_half],
                final_send.at[i], final_recv.at[plane_half], {"width": order[i]},
            )

    barrier = pltpu.get_barrier_semaphore()
    for k in range(1, m):
        pl.semaphore_signal(barrier, inc=1, device_id={"width": slabs[k]}, device_id_type=MESH)
    for k in range(1, n):
        pl.semaphore_signal(
            barrier, inc=1, device_id={"tour": lax.rem(t + k, n)}, device_id_type=MESH
        )
    for load in loads:
        load.wait()
    for h in both_halves:
        @pl.when(targets[h] == z)
        def _():
            text_all[0, z] = texts[:, spans[h]]
    pl.semaphore_wait(barrier, n + m - 2)

    for h in both_halves:
        @pl.when(elsewhere[h])
        def _():
            quarter[h].start()
    for p in both_halves:
        for k in (2, 1, 3):
            @pl.when(direct[k])
            def _():
                image[p, k].start()

    def pass_on(p):
        @pl.when(inner)
        def _():
            image_in[p, 2].wait_recv()
            relay[p].start()

    @pl.when(keeper)
    def _():
        for k in range(m):
            if k > 0:
                quarter_in[k].wait_recv()
            for r in range(1, chips):
                plane[r, k].start()
            share[0, k].start()

    spot = jnp.broadcast_to(matches[...].astype(jnp.float32), (half, rows)).T
    pass_on(0)

    @pl.when(keeper)
    def _():
        for k in range(m):
            for r in range(1, chips):
                plane_in[r, k].wait_recv()
                share[r, k].start()

    @pl.when(helper)
    def _():
        for k in range(m):
            for r in range(chips):
                plane_in[r, k].wait_recv()

    def text_slab(f):
        return jnp.concatenate([text_all[r, f] for r in range(chips)], axis=1)

    column = lax.broadcasted_iota(jnp.int32, (half, half), 1) + plane_half * half
    column = column.astype(jnp.float32)
    kept_label = jnp.where(keeper, 1.0, 0.0)
    counts = [len([s for s in range(-REACH, REACH + 1) if s % n == d]) for d in range(n)]
    times = []
    for r in range(chips):
        distance = lax.rem(t - keepers[r] + n, n)
        count = jnp.float32(0)
        for d in range(n):
            count = jnp.where(distance == d, jnp.float32(counts[d]), count)
        times.append(count)

    weights = []
    for p in both_halves:
        total = None
        for k in range(m):
            if k == 2:
                @pl.when(outer)
                def _():
                    image_in[p, 2].wait_recv()
            elif k > 0:
                image_in[p, k].wait_recv()
            term = cross_cols(image_all[slabs[k], :, spans[p]], text_slab(slabs[k]))
            total = term if total is None else total + term
        probs = jax.nn.sigmoid(temper * total + offset_bias)
        pieces = []
        for r in range(chips):
            piece = probs[:, r * half : (r + 1) * half]
            if r == 0:
                piece = piece - kept_label * (column == spot[spans[p]]).astype(jnp.float32)
            pieces.append(piece.astype(jnp.bfloat16).astype(jnp.float32) * times[r])
        pieces = jnp.concatenate(pieces, axis=1)
        weights.append(pieces.astype(jnp.bfloat16))
        turned = pieces.T.astype(jnp.bfloat16)

        for i, f in enumerate(order):
            term = jnp.dot(text_slab(f), turned, preferred_element_type=jnp.float32)
            if i < 2:
                @pl.when(outer)
                def _():
                    image_terms[p, i] = term.astype(jnp.bfloat16)
                    outer_out[p][i].start()

                @pl.when(inner)
                def _():
                    image_sums[p, i] = term
            elif i == 2:
                image_terms[p, 2] = term.astype(jnp.bfloat16)
                near_out[p].start()
            else:
                image_final[:, spans[p]] = term
        if p == 0:
            pass_on(1)
    weights = jnp.concatenate(weights, axis=0)

    def combine(p):
        @pl.when(inner)
        def _():
            for i in range(2):
                back_in[p][i].wait_recv()
                value = image_sums[p, i] + image_got[p, i].astype(jnp.float32)
                image_terms[p, i] = value.astype(jnp.bfloat16)
                inner_out[p][i].start()

    combine(0)
    for i, f in enumerate(order):
        term = jnp.dot(image_all[f], weights, preferred_element_type=jnp.float32)
        terms = [term[:, r * half : (r + 1) * half] for r in range(chips)]

        @pl.when(helper)
        def _():
            for r in range(chips):
                text_terms[i, r] = terms[r].astype(jnp.bfloat16)
            term_out[i].start()

        @pl.when(keeper)
        def _():
            term_out[i].wait_recv()
            for r in range(1, chips):
                both = terms[r] + term_got[i, r].astype(jnp.float32)
                text_terms[i, r] = both.astype(jnp.bfloat16)
                hop[i, r].start()
            text_own[i] = terms[0] + term_got[i, 0].astype(jnp.float32)

    combine(1)

    @pl.when(keeper)
    def _():
        for i in range(m):
            value = text_own[i]
            for r in range(1, chips):
                hop_in[i, r].wait_recv()
                value = value + text_got[i, r - 1].astype(jnp.float32)
            if i == m - 1:
                text_final[plane_half] = value
            else:
                text_sums[i] = value
                final[i].start()

    stores = []
    for p in both_halves:
        value = image_final[:, spans[p]]
        for i in (2, 3):
            back_in[p][i].wait_recv()
            value = value + image_got[p, i].astype(jnp.float32)
        image_final[:, spans[p]] = value
        stores.append(
            pltpu.make_async_copy(
                image_final.at[:, spans[p]], grad_image.at[:, spans[p]], store_sem.at[p]
            )
        )
        stores[-1].start()
    for h in both_halves:
        @pl.when(elsewhere[h])
        def _():
            final_in[h].wait_recv()
            quarter[h].wait_send()
        stores.append(
            pltpu.make_async_copy(
                text_final.at[h], grad_text.at[:, spans[h]], store_sem.at[halves + h]
            )
        )
        stores[-1].start()
    for p in both_halves:
        for k in range(1, m):
            @pl.when(direct[k])
            def _():
                image[p, k].wait_send()
        near_out[p].wait_send()

        @pl.when(outer)
        def _():
            for copy in outer_out[p]:
                copy.wait_send()

        @pl.when(inner)
        def _():
            for copy in [relay[p]] + inner_out[p]:
                copy.wait_send()

    @pl.when(keeper)
    def _():
        for group in (plane, share, hop, final):
            for copy in group.values():
                copy.wait_send()

    @pl.when(helper)
    def _():
        for copy in term_out.values():
            copy.wait_send()

    for store in stores:
        store.wait()


def whole(images, texts, matches, scale, shift_bias):
    n, m = lax.axis_size("tour"), lax.axis_size("width")
    rows, width = images.shape
    chips, halves = n // 2, m // 2
    half = rows // halves
    hbm = pl.BlockSpec(memory_space=pltpu.HBM)
    smem = pl.BlockSpec(memory_space=pltpu.SMEM)
    out = jax.ShapeDtypeStruct((width, rows), jnp.float32)

    def dma(*shape):
        return pltpu.SemaphoreType.DMA(shape)

    def narrow(*shape):
        return pltpu.VMEM(shape, jnp.bfloat16)

    def wide(*shape):
        return pltpu.VMEM(shape, jnp.float32)

    grads = pl.pallas_call(
        functools.partial(kernel, n, m),
        out_shape=(out, out),
        in_specs=[hbm, hbm, hbm, smem, smem],
        out_specs=(hbm, hbm),
        scratch_shapes=[
            narrow(width, rows), pltpu.VMEM((1, rows), jnp.int32), narrow(m, width, rows),
            narrow(chips, m, width, half), narrow(m, chips, width, half),
            narrow(m, chips, width, half), narrow(m, chips - 1, width, half),
            wide(m, width, half), wide(m - 1, width, half), wide(halves, width, half),
            narrow(halves, 3, width, half), wide(halves, 2, width, half),
            narrow(halves, 4, width, half), wide(width, rows),
            dma(3), dma(2 * halves), dma(halves), dma(halves), dma(m), dma(halves, m), dma(halves, m),
            dma(chips, m), dma(chips, m), dma(chips, m), dma(m), dma(m), dma(m, chips), dma(m, chips),
            dma(halves, 3), dma(halves, 4), dma(m), dma(halves),
        ],
        compiler_params=pltpu.CompilerParams(
            collective_id=0, has_side_effects=True, vmem_limit_bytes=60 * 1024 * 1024
        ),
    )(images.T, texts.T, matches, scale, shift_bias)
    return tuple(scale[0] * grad.T for grad in grads)


def solution(mesh):
    placed = (P("tour", "width"), P("tour", "width"), P("tour", None), P(), P())
    n, m = mesh.shape["tour"], mesh.shape["width"]
    body = whole if n <= 2 * REACH + 1 and n % 2 == 0 and m == 4 else band
    return jax.shard_map(
        body,
        mesh=mesh,
        in_specs=placed,
        out_specs=(P("tour", "width"), P("tour", "width")),
        check_vma=False,
    )
```

time: 54.3 us -> 51.2 us (0.943)
  the two profiles are of different devices: /device:TPU:16 before, /device:TPU:0 now
where the time goes in v5:
time: 51.2 us; the launch traced here: 50.5 us
  Pallas kernels  46.7 us (91%)
  between operations  1.93 us (4%)
  other arithmetic  1.9 us (4%)
    pallas_call x1, Pallas kernels, whole(): pl.pallas_call(functools.partial(kernel, n, m), out_shape=(out, out), in_...  46.7 us
    mul x1, other arithmetic, whole(): return tuple((scale[0] * grad.T for grad in grads))  1.9 us

profile of v5, /device:TPU:0, one launch (start us, length us, event | category | flops | bytes accessed | tf_op | source)
XLA Modules:
  0.0 50.5 jit_solution(12688690340494948089)
XLA Ops:
  1.9 46.7 %shard_map.68 = (f32[288,256]{1,0:T(8,128)}, f32[288,256]{1,0:T(8,128)}) custom-call(bf16[288,256]{1,0:T(8,128)(2,1)} %bitcast.8, bf16[288,256]{1,0:T(8,128)(2,1)} %bitcast.9, s32[1,256]{1,0:T(1,128)} %matches_in.1, f32[1]{0:T(128)} %copy.7.scale, f32[1]{0:T(128)S(6)} %copy.8.shift_bias), custom_call_target="tpu_custom_call" | custom-call | tf_op jit(solution)/shard_map/pallas_call | solution.py:416
  48.6 1.9 %multiply_bitcast_fusion = (f32[256,288]{0,1:T(8,128)}, f32[256,288]{0,1:T(8,128)}) fusion(f32[288,256]{1,0:T(8,128)} %get-tuple-element.5, f32[]{:T(128)} %bitcast.7, f32[288,256]{1,0:T(8,128)} %get-tuple-element.4), kind=kLoop, calls=%fused_computation | loop fusion | flops 147456 | bytes 1179652 | tf_op jit(solution)/shard_map/mul | solution.py:436

commit v6 on v5

--- a/solution.py
+++ b/solution.py
@@ -65,7 +65,7 @@
 
 def kernel(
     n, m, images_in, texts_in, matches_in, scale, shift_bias, grad_image, grad_text,
-    texts, matches, image_all, text_all, text_terms, term_got, text_got, text_own, text_sums, text_final,
+    texts, matches, image_all, text_all, text_terms, term_got, hop_terms, text_got, text_own, text_sums, text_final,
     image_terms, image_sums, image_got, image_final,
     load_sem, store_sem, relay_send, quarter_send, quarter_recv, image_send, image_recv,
     plane_send, plane_recv, share_send, term_send, term_recv, hop_send, hop_recv,
@@ -79,13 +79,15 @@
     temper, offset_bias = scale[0], shift_bias[0]
     core, chip = lax.rem(t, cores), lax.div(t, cores)
     plane_core, plane_half = lax.div(z, halves), lax.rem(z, halves)
-    keeper = core == plane_core
-    helper = core != plane_core
     sibling = chip * cores + (cores - 1 - core)
     slabs = [lax.rem(z + k, m) for k in range(m)]
     keepers = [lax.rem(chip + r, chips) * cores + plane_core for r in range(chips)]
+    peers = [lax.rem(chip + r, chips) * cores + core for r in range(chips)]
     targets = [core * halves + h for h in range(halves)]
-    elsewhere = [target != z for target in targets]
+    same_core = lax.rem(z, cores) == core
+    local = [jnp.logical_and(target == z, same_core) for target in targets]
+    elsewhere = [jnp.logical_not(here) for here in local]
+    landing, origin = chip * cores + lax.rem(z, cores), chip * cores + plane_core
     both_halves = range(halves)
     spans = [slice(p * half, (p + 1) * half) for p in both_halves]
     outer = jnp.logical_or(z == 0, z == m - 1)
@@ -96,6 +98,11 @@
     far_outer = jnp.where(low, m - 1, 0)
     direct = [jnp.logical_or(inner, f != far_outer) for f in slabs]
     order = (far_outer, far_inner, partner, z)
+    far_start = jnp.where(low, halves, 0)
+    mine = [far_start + core, halves - far_start + core]
+    theirs = [far_start + cores - 1 - core, halves - far_start + cores - 1 - core]
+    home = [jnp.logical_and(f == z, plane_core == core) for f in mine]
+    abroad = [jnp.logical_not(here) for here in home]
 
     loads = [
         pltpu.make_async_copy(images_in, image_all.at[z], load_sem.at[0]),
@@ -117,21 +124,20 @@
     quarter = [
         remote(
             texts.at[:, spans[h]], text_all.at[0, z],
-            quarter_send.at[h], quarter_recv.at[z], {"width": targets[h]},
+            quarter_send.at[h], quarter_recv.at[z], {"tour": landing, "width": targets[h]},
         )
         for h in both_halves
     ]
     image, image_in, quarter_in, final = {}, {}, {}, {}
-    plane, plane_in, share, term_out, hop, hop_in = {}, {}, {}, {}, {}, {}
+    plane, plane_in, share, share_in, term_out, hop, hop_in = {}, {}, {}, {}, {}, {}, {}
     for k in range(1, m):
         f = slabs[k]
-        quarter_in[k] = arriving(text_all.at[0, f], quarter_recv.at[f])
         for p in both_halves:
-            mine, theirs = image_all.at[z, :, spans[p]], image_all.at[f, :, spans[p]]
+            sent, comes = image_all.at[z, :, spans[p]], image_all.at[f, :, spans[p]]
             image[p, k] = remote(
-                mine, mine, image_send.at[p, k], image_recv.at[p, z], {"width": f}
-            )
-            image_in[p, k] = arriving(theirs, image_recv.at[p, f])
+                sent, sent, image_send.at[p, k], image_recv.at[p, z], {"width": f}
+            )
+            image_in[p, k] = arriving(comes, image_recv.at[p, f])
     relay, near_out, outer_out, inner_out, back_in = [], [], [], [], []
     for p in both_halves:
         passed = image_all.at[far_outer, :, spans[p]]
@@ -152,49 +158,49 @@
         inner_out.append([back(0, 3, far_outer), back(1, 3, far_inner)])
         back_in.append([arriving(image_got.at[p, i], back_recv.at[p, i]) for i in range(4)])
     final_in = [arriving(text_final.at[h], final_recv.at[h]) for h in both_halves]
-    for r in range(chips):
-        for k in range(m):
-            f = slabs[k]
-            plane_in[r, k] = arriving(text_all.at[r, f], plane_recv.at[r, f])
-            share[r, k] = remote(
-                text_all.at[r, f], text_all.at[r, f], share_send.at[r, k], plane_recv.at[r, f],
+    for j in range(2):
+        f, g = mine[j], theirs[j]
+        quarter_in[j] = arriving(text_all.at[0, f], quarter_recv.at[f])
+        term_out[j] = remote(
+            text_terms.at[j], term_got.at[j], term_send.at[j], term_recv.at[j], {"tour": sibling}
+        )
+        final[j] = remote(
+            text_sums.at[j], text_final.at[plane_half], final_send.at[j], final_recv.at[plane_half],
+            {"tour": origin, "width": f},
+        )
+        for r in range(chips):
+            plane_in[r, j] = arriving(text_all.at[r, f], plane_recv.at[r, f])
+            share_in[r, j] = arriving(text_all.at[r, g], plane_recv.at[r, g])
+            share[r, j] = remote(
+                text_all.at[r, f], text_all.at[r, f], share_send.at[r, j], plane_recv.at[r, f],
                 {"tour": sibling},
             )
             if r > 0:
-                plane[r, k] = remote(
+                plane[r, j] = remote(
                     text_all.at[0, f], text_all.at[chips - r, f],
-                    plane_send.at[r, k], plane_recv.at[chips - r, f], {"tour": keepers[r]},
+                    plane_send.at[r, j], plane_recv.at[chips - r, f], {"tour": peers[r]},
                 )
-    for i in range(m):
-        term_out[i] = remote(
-            text_terms.at[i], term_got.at[i], term_send.at[i], term_recv.at[i], {"tour": sibling}
-        )
-        for r in range(1, chips):
-            hop[i, r] = remote(
-                text_terms.at[i, r], text_got.at[i, chips - r - 1],
-                hop_send.at[i, r], hop_recv.at[i, chips - r], {"tour": keepers[r]},
-            )
-            hop_in[i, r] = arriving(text_got.at[i, r - 1], hop_recv.at[i, r])
-        if i < m - 1:
-            final[i] = remote(
-                text_sums.at[i], text_final.at[plane_half],
-                final_send.at[i], final_recv.at[plane_half], {"width": order[i]},
-            )
+                hop[r, j] = remote(
+                    hop_terms.at[j, r - 1], text_got.at[j, chips - r - 1],
+                    hop_send.at[r, j], hop_recv.at[chips - r, j], {"tour": peers[r]},
+                )
+                hop_in[r, j] = arriving(text_got.at[j, r - 1], hop_recv.at[r, j])
 
     barrier = pltpu.get_barrier_semaphore()
     for k in range(1, m):
         pl.semaphore_signal(barrier, inc=1, device_id={"width": slabs[k]}, device_id_type=MESH)
-    for k in range(1, n):
         pl.semaphore_signal(
-            barrier, inc=1, device_id={"tour": lax.rem(t + k, n)}, device_id_type=MESH
-        )
+            barrier, inc=1, device_id={"tour": sibling, "width": slabs[k]}, device_id_type=MESH
+        )
+    for other in peers[1:] + [sibling]:
+        pl.semaphore_signal(barrier, inc=1, device_id={"tour": other}, device_id_type=MESH)
     for load in loads:
         load.wait()
     for h in both_halves:
-        @pl.when(targets[h] == z)
+        @pl.when(local[h])
         def _():
             text_all[0, z] = texts[:, spans[h]]
-    pl.semaphore_wait(barrier, n + m - 2)
+    pl.semaphore_wait(barrier, 2 * (m - 1) + chips)
 
     for h in both_halves:
         @pl.when(elsewhere[h])
@@ -212,37 +218,31 @@
             image_in[p, 2].wait_recv()
             relay[p].start()
 
-    @pl.when(keeper)
-    def _():
-        for k in range(m):
-            if k > 0:
-                quarter_in[k].wait_recv()
-            for r in range(1, chips):
-                plane[r, k].start()
-            share[0, k].start()
+    for j in (1, 0):
+        @pl.when(abroad[j])
+        def _():
+            quarter_in[j].wait_recv()
+        for r in range(1, chips):
+            plane[r, j].start()
+        share[0, j].start()
 
     spot = jnp.broadcast_to(matches[...].astype(jnp.float32), (half, rows)).T
     pass_on(0)
 
-    @pl.when(keeper)
-    def _():
-        for k in range(m):
-            for r in range(1, chips):
-                plane_in[r, k].wait_recv()
-                share[r, k].start()
-
-    @pl.when(helper)
-    def _():
-        for k in range(m):
-            for r in range(chips):
-                plane_in[r, k].wait_recv()
+    for j in (1, 0):
+        for r in range(1, chips):
+            plane_in[r, j].wait_recv()
+            share[r, j].start()
+    for j in (1, 0):
+        for r in range(chips):
+            share_in[r, j].wait_recv()
 
     def text_slab(f):
         return jnp.concatenate([text_all[r, f] for r in range(chips)], axis=1)
 
     column = lax.broadcasted_iota(jnp.int32, (half, half), 1) + plane_half * half
     column = column.astype(jnp.float32)
-    kept_label = jnp.where(keeper, 1.0, 0.0)
+    kept_label = jnp.where(core == plane_core, 1.0, 0.0)
     counts = [len([s for s in range(-REACH, REACH + 1) if s % n == d]) for d in range(n)]
     times = []
     for r in range(chips):
@@ -305,39 +305,40 @@
                 inner_out[p][i].start()
 
     combine(0)
-    for i, f in enumerate(order):
+
+    def text_term(f):
         term = jnp.dot(image_all[f], weights, preferred_element_type=jnp.float32)
-        terms = [term[:, r * half : (r + 1) * half] for r in range(chips)]
-
-        @pl.when(helper)
-        def _():
-            for r in range(chips):
-                text_terms[i, r] = terms[r].astype(jnp.bfloat16)
-            term_out[i].start()
-
-        @pl.when(keeper)
-        def _():
-            term_out[i].wait_recv()
-            for r in range(1, chips):
-                both = terms[r] + term_got[i, r].astype(jnp.float32)
-                text_terms[i, r] = both.astype(jnp.bfloat16)
-                hop[i, r].start()
-            text_own[i] = terms[0] + term_got[i, 0].astype(jnp.float32)
+        return [term[:, r * half : (r + 1) * half] for r in range(chips)]
+
+    for j in range(2):
+        terms = text_term(theirs[j])
+        for r in range(chips):
+            text_terms[j, r] = terms[r].astype(jnp.bfloat16)
+        term_out[j].start()
+    for j in range(2):
+        terms = text_term(mine[j])
+        term_out[j].wait_recv()
+        for r in range(1, chips):
+            both = terms[r] + term_got[j, r].astype(jnp.float32)
+            hop_terms[j, r - 1] = both.astype(jnp.bfloat16)
+            hop[r, j].start()
+        text_own[j] = terms[0] + term_got[j, 0].astype(jnp.float32)
 
     combine(1)
-
-    @pl.when(keeper)
-    def _():
-        for i in range(m):
-            value = text_own[i]
-            for r in range(1, chips):
-                hop_in[i, r].wait_recv()
-                value = value + text_got[i, r - 1].astype(jnp.float32)
-            if i == m - 1:
-                text_final[plane_half] = value
-            else:
-                text_sums[i] = value
-                final[i].start()
+    for j in range(2):
+        value = text_own[j]
+        for r in range(1, chips):
+            hop_in[r, j].wait_recv()
+            value = value + text_got[j, r - 1].astype(jnp.float32)
+        text_sums[j] = value
+
+        @pl.when(home[j])
+        def _():
+            text_final[plane_half] = text_sums[j]
+
+        @pl.when(abroad[j])
+        def _():
+            final[j].start()
 
     stores = []
     for p in both_halves:
@@ -380,16 +381,13 @@
             for copy in [relay[p]] + inner_out[p]:
                 copy.wait_send()
 
-    @pl.when(keeper)
-    def _():
-        for group in (plane, share, hop, final):
-            for copy in group.values():
-                copy.wait_send()
-
-    @pl.when(helper)
-    def _():
-        for copy in term_out.values():
+    for group in (plane, share, hop, term_out):
+        for copy in group.values():
             copy.wait_send()
+    for j in range(2):
+        @pl.when(abroad[j])
+        def _():
+            final[j].wait_send()
 
     for store in stores:
         store.wait()
@@ -420,14 +418,15 @@
         out_specs=(hbm, hbm),
         scratch_shapes=[
             narrow(width, rows), pltpu.VMEM((1, rows), jnp.int32), narrow(m, width, rows),
-            narrow(chips, m, width, half), narrow(m, chips, width, half),
-            narrow(m, chips, width, half), narrow(m, chips - 1, width, half),
-            wide(m, width, half), wide(m - 1, width, half), wide(halves, width, half),
+            narrow(chips, m, width, half), narrow(2, chips, width, half),
+            narrow(2, chips, width, half), narrow(2, chips - 1, width, half),
+            narrow(2, chips - 1, width, half),
+            wide(2, width, half), wide(2, width, half), wide(halves, width, half),
             narrow(halves, 3, width, half), wide(halves, 2, width, half),
             narrow(halves, 4, width, half), wide(width, rows),
             dma(3), dma(2 * halves), dma(halves), dma(halves), dma(m), dma(halves, m), dma(halves, m),
-            dma(chips, m), dma(chips, m), dma(chips, m), dma(m), dma(m), dma(m, chips), dma(m, chips),
-            dma(halves, 3), dma(halves, 4), dma(m), dma(halves),
+            dma(chips, 2), dma(chips, m), dma(chips, 2), dma(2), dma(2), dma(chips, 2), dma(chips, 2),
+            dma(halves, 3), dma(halves, 4), dma(2), dma(halves),
         ],
         compiler_params=pltpu.CompilerParams(
             collective_id=0, has_side_effects=True, vmem_limit_bytes=60 * 1024 * 1024

time: 51.2 us -> 47.6 us (0.930)
  the two profiles are of different devices: /device:TPU:0 before, /device:TPU:8 now
where the time goes in v6:
time: 47.6 us; the launch traced here: 47.4 us
  Pallas kernels  43.6 us (92%)
  between operations  1.93 us (4%)
  other arithmetic  1.9 us (4%)
    pallas_call x1, Pallas kernels, whole(): pl.pallas_call(functools.partial(kernel, n, m), out_shape=(out, out), in_...  43.6 us
    mul x1, other arithmetic, whole(): return tuple((scale[0] * grad.T for grad in grads))  1.9 us

profile of v6, /device:TPU:8, one launch (start us, length us, event | category | flops | bytes accessed | tf_op | source)
XLA Modules:
  0.0 47.4 jit_solution(14002571364332908889)
XLA Ops:
  1.9 43.6 %shard_map.68 = (f32[288,256]{1,0:T(8,128)}, f32[288,256]{1,0:T(8,128)}) custom-call(bf16[288,256]{1,0:T(8,128)(2,1)} %bitcast.8, bf16[288,256]{1,0:T(8,128)(2,1)} %bitcast.9, s32[1,256]{1,0:T(1,128)} %matches_in.1, f32[1]{0:T(128)} %copy.7.scale, f32[1]{0:T(128)S(6)} %copy.8.shift_bias), custom_call_target="tpu_custom_call" | custom-call | tf_op jit(solution)/shard_map/pallas_call | solution.py:414
  45.5 1.9 %multiply_bitcast_fusion = (f32[256,288]{0,1:T(8,128)}, f32[256,288]{0,1:T(8,128)}) fusion(f32[288,256]{1,0:T(8,128)} %get-tuple-element.5, f32[]{:T(128)} %bitcast.7, f32[288,256]{1,0:T(8,128)} %get-tuple-element.4), kind=kLoop, calls=%fused_computation | loop fusion | flops 147456 | bytes 1179652 | tf_op jit(solution)/shard_map/mul | solution.py:435

commit v7 on v6

--- a/solution.py
+++ b/solution.py
@@ -72,7 +72,7 @@
     back_send, back_recv, final_send, final_recv,
 ):
     t, z = lax.axis_index("tour"), lax.axis_index("width")
-    width, rows = texts.shape
+    width, rows = images_in.shape
     cores = 2
     halves, chips = m // cores, n // cores
     half = rows // halves
@@ -104,11 +104,12 @@
     home = [jnp.logical_and(f == z, plane_core == core) for f in mine]
     abroad = [jnp.logical_not(here) for here in home]
 
-    loads = [
-        pltpu.make_async_copy(images_in, image_all.at[z], load_sem.at[0]),
-        pltpu.make_async_copy(texts_in, texts, load_sem.at[1]),
-        pltpu.make_async_copy(matches_in, matches, load_sem.at[2]),
-    ]
+    loads = [pltpu.make_async_copy(matches_in, matches, load_sem.at[2 * halves])]
+    for p in both_halves:
+        loads += [
+            pltpu.make_async_copy(texts_in.at[:, spans[p]], texts.at[p], load_sem.at[halves + p]),
+            pltpu.make_async_copy(images_in.at[:, spans[p]], image_all.at[z, p], load_sem.at[p]),
+        ]
     for load in loads:
         load.start()
 
@@ -123,7 +124,7 @@
 
     quarter = [
         remote(
-            texts.at[:, spans[h]], text_all.at[0, z],
+            texts.at[h], text_all.at[0, z],
             quarter_send.at[h], quarter_recv.at[z], {"tour": landing, "width": targets[h]},
         )
         for h in both_halves
@@ -133,14 +134,14 @@
     for k in range(1, m):
         f = slabs[k]
         for p in both_halves:
-            sent, comes = image_all.at[z, :, spans[p]], image_all.at[f, :, spans[p]]
+            sent, comes = image_all.at[z, p], image_all.at[f, p]
             image[p, k] = remote(
                 sent, sent, image_send.at[p, k], image_recv.at[p, z], {"width": f}
             )
             image_in[p, k] = arriving(comes, image_recv.at[p, f])
     relay, near_out, outer_out, inner_out, back_in = [], [], [], [], []
     for p in both_halves:
-        passed = image_all.at[far_outer, :, spans[p]]
+        passed = image_all.at[far_outer, p]
         relay.append(
             remote(
                 passed, passed, relay_send.at[p], image_recv.at[p, far_outer], {"width": partner}
@@ -199,14 +200,15 @@
     for h in both_halves:
         @pl.when(local[h])
         def _():
-            text_all[0, z] = texts[:, spans[h]]
+            text_all[0, z] = texts[h]
     pl.semaphore_wait(barrier, 2 * (m - 1) + chips)
 
     for h in both_halves:
         @pl.when(elsewhere[h])
         def _():
             quarter[h].start()
-    for p in both_halves:
+
+    def send_images(p):
         for k in (2, 1, 3):
             @pl.when(direct[k])
             def _():
@@ -226,7 +228,13 @@
             plane[r, j].start()
         share[0, j].start()
 
+    send_images(0)
     spot = jnp.broadcast_to(matches[...].astype(jnp.float32), (half, rows)).T
+    for k in range(1, m):
+        @pl.when(direct[k])
+        def _():
+            image[0, k].wait_send()
+    send_images(1)
     pass_on(0)
 
     for j in (1, 0):
@@ -262,7 +270,7 @@
                     image_in[p, 2].wait_recv()
             elif k > 0:
                 image_in[p, k].wait_recv()
-            term = cross_cols(image_all[slabs[k], :, spans[p]], text_slab(slabs[k]))
+            term = cross_cols(image_all[slabs[k], p], text_slab(slabs[k]))
             total = term if total is None else total + term
         probs = jax.nn.sigmoid(temper * total + offset_bias)
         pieces = []
@@ -304,10 +312,9 @@
                 image_terms[p, i] = value.astype(jnp.bfloat16)
                 inner_out[p][i].start()
 
-    combine(0)
-
     def text_term(f):
-        term = jnp.dot(image_all[f], weights, preferred_element_type=jnp.float32)
+        slab = jnp.concatenate([image_all[f, p] for p in both_halves], axis=1)
+        term = jnp.dot(slab, weights, preferred_element_type=jnp.float32)
         return [term[:, r * half : (r + 1) * half] for r in range(chips)]
 
     for j in range(2):
@@ -315,6 +322,7 @@
         for r in range(chips):
             text_terms[j, r] = terms[r].astype(jnp.bfloat16)
         term_out[j].start()
+    combine(0)
     for j in range(2):
         terms = text_term(mine[j])
         term_out[j].wait_recv()
@@ -365,10 +373,11 @@
         )
         stores[-1].start()
     for p in both_halves:
-        for k in range(1, m):
-            @pl.when(direct[k])
-            def _():
-                image[p, k].wait_send()
+        if p == 1:
+            for k in range(1, m):
+                @pl.when(direct[k])
+                def _():
+                    image[1, k].wait_send()
         near_out[p].wait_send()
 
         @pl.when(outer)
@@ -417,14 +426,15 @@
         in_specs=[hbm, hbm, hbm, smem, smem],
         out_specs=(hbm, hbm),
         scratch_shapes=[
-            narrow(width, rows), pltpu.VMEM((1, rows), jnp.int32), narrow(m, width, rows),
+            narrow(halves, width, half), pltpu.VMEM((1, rows), jnp.int32),
+            narrow(m, halves, width, half),
             narrow(chips, m, width, half), narrow(2, chips, width, half),
             narrow(2, chips, width, half), narrow(2, chips - 1, width, half),
             narrow(2, chips - 1, width, half),
             wide(2, width, half), wide(2, width, half), wide(halves, width, half),
             narrow(halves, 3, width, half), wide(halves, 2, width, half),
             narrow(halves, 4, width, half), wide(width, rows),
-            dma(3), dma(2 * halves), dma(halves), dma(halves), dma(m), dma(halves, m), dma(halves, m),
+            dma(2 * halves + 1), dma(2 * halves), dma(halves), dma(halves), dma(m), dma(halves, m), dma(halves, m),
             dma(chips, 2), dma(chips, m), dma(chips, 2), dma(2), dma(2), dma(chips, 2), dma(chips, 2),
             dma(halves, 3), dma(halves, 4), dma(2), dma(halves),
         ],

time: 47.6 us -> 45.3 us (0.952)
  the two profiles are of different devices: /device:TPU:8 before, /device:TPU:0 now
where the time goes in v7:
time: 45.3 us; the launch traced here: 44.6 us
  Pallas kernels  40.8 us (90%)
  between operations  1.93 us (4%)
  other arithmetic  1.9 us (4%)
    pallas_call x1, Pallas kernels, whole(): pl.pallas_call(functools.partial(kernel, n, m), out_shape=(out, out), in_...  40.8 us
    mul x1, other arithmetic, whole(): return tuple((scale[0] * grad.T for grad in grads))  1.9 us

profile of v7, /device:TPU:0, one launch (start us, length us, event | category | flops | bytes accessed | tf_op | source)
XLA Modules:
  0.0 44.6 jit_solution(6435901735768533684)
XLA Ops:
  1.9 40.8 %shard_map.68 = (f32[288,256]{1,0:T(8,128)}, f32[288,256]{1,0:T(8,128)}) custom-call(bf16[288,256]{1,0:T(8,128)(2,1)} %bitcast.8, bf16[288,256]{1,0:T(8,128)(2,1)} %bitcast.9, s32[1,256]{1,0:T(1,128)} %matches_in.1, f32[1]{0:T(128)} %copy.7.scale, f32[1]{0:T(128)S(6)} %copy.8.shift_bias), custom_call_target="tpu_custom_call" | custom-call | tf_op jit(solution)/shard_map/pallas_call | solution.py:423
  42.7 1.9 %multiply_bitcast_fusion = (f32[256,288]{0,1:T(8,128)}, f32[256,288]{0,1:T(8,128)}) fusion(f32[288,256]{1,0:T(8,128)} %get-tuple-element.5, f32[]{:T(128)} %bitcast.7, f32[288,256]{1,0:T(8,128)} %get-tuple-element.4), kind=kLoop, calls=%fused_computation | loop fusion | flops 147456 | bytes 1179652 | tf_op jit(solution)/shard_map/mul | solution.py:445

commit v8 on v7

--- a/solution.py
+++ b/solution.py
@@ -260,6 +260,14 @@
             count = jnp.where(distance == d, jnp.float32(counts[d]), count)
         times.append(count)
 
+    def image_term(i, turned):
+        return jnp.dot(text_slab(order[i]), turned, preferred_element_type=jnp.float32)
+
+    def near_terms(p, turned):
+        image_terms[p, 2] = image_term(2, turned).astype(jnp.bfloat16)
+        near_out[p].start()
+        image_final[:, spans[p]] = image_term(3, turned)
+
     weights = []
     for p in both_halves:
         total = None
@@ -283,22 +291,19 @@
         weights.append(pieces.astype(jnp.bfloat16))
         turned = pieces.T.astype(jnp.bfloat16)
 
-        for i, f in enumerate(order):
-            term = jnp.dot(text_slab(f), turned, preferred_element_type=jnp.float32)
-            if i < 2:
-                @pl.when(outer)
-                def _():
-                    image_terms[p, i] = term.astype(jnp.bfloat16)
-                    outer_out[p][i].start()
-
-                @pl.when(inner)
-                def _():
-                    image_sums[p, i] = term
-            elif i == 2:
-                image_terms[p, 2] = term.astype(jnp.bfloat16)
-                near_out[p].start()
-            else:
-                image_final[:, spans[p]] = term
+        for i in range(2):
+            term = image_term(i, turned)
+
+            @pl.when(outer)
+            def _():
+                image_terms[p, i] = term.astype(jnp.bfloat16)
+                outer_out[p][i].start()
+
+            @pl.when(inner)
+            def _():
+                image_sums[p, i] = term
+        if p == 0:
+            near_terms(p, turned)
         if p == 0:
             pass_on(1)
     weights = jnp.concatenate(weights, axis=0)
@@ -329,9 +334,15 @@
         for r in range(1, chips):
             both = terms[r] + term_got[j, r].astype(jnp.float32)
             hop_terms[j, r - 1] = both.astype(jnp.bfloat16)
-            hop[r, j].start()
+            if j == 0:
+                hop[r, j].start()
         text_own[j] = terms[0] + term_got[j, 0].astype(jnp.float32)
 
+    near_terms(1, turned)
+    for r in range(1, chips):
+        hop[r, 0].wait_send()
+    for r in range(1, chips):
+        hop[r, 1].start()
     combine(1)
     for j in range(2):
         value = text_own[j]
@@ -390,7 +401,9 @@
             for copy in [relay[p]] + inner_out[p]:
                 copy.wait_send()
 
-    for group in (plane, share, hop, term_out):
+    for r in range(1, chips):
+        hop[r, 1].wait_send()
+    for group in (plane, share, term_out):
         for copy in group.values():
             copy.wait_send()
     for j in range(2):

time: 45.3 us -> 46.3 us (1.022); the launches traced: 44.6 us -> 46.1 us
  Pallas kernels: 40.8 us -> 42.3 us
    pallas_call x1, Pallas kernels: 40.8 us -> 42.3 us  [whole(): pl.pallas_call(functools.partial(kernel, n, m), out_shape=(out, out), in_...]
where the time goes in v8:
time: 46.3 us; the launch traced here: 46.1 us
  Pallas kernels  42.3 us (91%)
  between operations  1.93 us (4%)
  other arithmetic  1.9 us (4%)
    pallas_call x1, Pallas kernels, whole(): pl.pallas_call(functools.partial(kernel, n, m), out_shape=(out, out), in_...  42.3 us
    mul x1, other arithmetic, whole(): return tuple((scale[0] * grad.T for grad in grads))  1.9 us

profile of v8, /device:TPU:0, one launch (start us, length us, event | category | flops | bytes accessed | tf_op | source)
XLA Modules:
  0.0 46.1 jit_solution(18288047040331963550)
XLA Ops:
  1.9 42.3 %shard_map.68 = (f32[288,256]{1,0:T(8,128)}, f32[288,256]{1,0:T(8,128)}) custom-call(bf16[288,256]{1,0:T(8,128)(2,1)} %bitcast.8, bf16[288,256]{1,0:T(8,128)(2,1)} %bitcast.9, s32[1,256]{1,0:T(1,128)} %matches_in.1, f32[1]{0:T(128)} %copy.7.scale, f32[1]{0:T(128)S(6)} %copy.8.shift_bias), custom_call_target="tpu_custom_call" | custom-call | tf_op jit(solution)/shard_map/pallas_call | solution.py:436
  44.2 1.9 %multiply_bitcast_fusion = (f32[256,288]{0,1:T(8,128)}, f32[256,288]{0,1:T(8,128)}) fusion(f32[288,256]{1,0:T(8,128)} %get-tuple-element.5, f32[]{:T(128)} %bitcast.7, f32[288,256]{1,0:T(8,128)} %get-tuple-element.4), kind=kLoop, calls=%fused_computation | loop fusion | flops 147456 | bytes 1179652 | tf_op jit(solution)/shard_map/mul | solution.py:458
